TPU v7x, 32 devices: a whole 2x2x4 slice. The times are simulated.
32 devices in a mesh: wide: 8 (over z, x), narrow: 4 (over y, core).
Axes of the slice: x: 2, y: 2, z: 4, core: 2. Of those that a mesh axis runs over, the one named last changes fastest.
Arguments:
- object_field: float32 [2, 2048, 2048], P(None, 'narrow', 'wide'), may hold values from -6 to 6
- probe: float32 [4, 2, 256, 256], replicated, may hold values from -3 to 3
- amplitudes: float32 [256, 256, 256], P(('wide', 'narrow')), may hold values from 0.5 to 4
- offsets: int32 [256, 2], P(('wide', 'narrow')), may hold values from 0 to 1792, as said below
- live: int32 [32], P(('wide', 'narrow')), may hold values from 1 to 8, as said below
Outputs:
- object_grad: float32 [2, 2048, 2048], P(None, 'narrow', 'wide')
- probe_grad: float32 [4, 2, 256, 256], replicated
Inputs may be any that keep to these rules, and one draw needn't show every extreme that they name: `offsets`: the patch of every slot (used or not) lies wholly inside the object, and starts inside the object tile of 512 rows and 256 columns that holds the same mesh place as the slot: slot p with b = p // 8, row tile b % (2048 / 512) and column tile b // (2048 / 512). Block b of 8 slots uses its first live[b] slots; in every draw some block uses all 8.
All inputs are finite; a program needn't handle non-finite values.
Results may differ from a plain program's by a relative error of at most 0.005.
Values sent between devices are 32-bit elements; how exact they have to be, the bound alone decides.
No kernel may reach another device: no remote copies, remote signals or barrier semaphores. Data moves between devices by JAX's collectives and lax.ppermute only.
A program may use at most 128 MiB of HBM per device.

v0:
```python
import math

import jax
import jax.numpy as jnp
from jax import lax
from jax.sharding import PartitionSpec as P


def shifted(value, axis, steps):
    count = lax.axis_size(axis)
    first, last = (max(0, -steps), min(count, count - steps))
    return lax.ppermute(value, axis, [(source, source + steps) for source in range(first, last)])


def dft_blocks(extent):
    freq = jnp.arange(extent, dtype=jnp.int32)
    phases = freq[:, None] * freq[None, :] % extent
    angles = phases.astype(jnp.float32) * (2.0 * math.pi / extent)
    scale = 1.0 / math.sqrt(extent)
    cosine = jnp.cos(angles) * scale
    sine = jnp.sin(angles) * scale
    forward = jnp.concatenate(
        [jnp.concatenate([cosine, sine], 1), jnp.concatenate([-sine, cosine], 1)], 0
    )
    backward = jnp.concatenate(
        [jnp.concatenate([cosine, -sine], 1), jnp.concatenate([sine, cosine], 1)], 0
    )
    return (forward.astype(jnp.bfloat16), backward.astype(jnp.bfloat16))


def left_apply(block, waves):
    modes = waves.shape[0]
    extent = waves.shape[2]
    stacked = waves.reshape(modes, 2 * extent, waves.shape[3])
    result = jnp.einsum("ab,kbc->kac", block, stacked, preferred_element_type=jnp.float32)
    return result.reshape(modes, 2, extent, waves.shape[3])


def slot_gradients(window, probe, amplitude, forward, backward):
    probe_re = probe[:, 0]
    probe_im = probe[:, 1]
    object_re = window[0]
    object_im = window[1]
    waves = jnp.stack(
        [probe_re * object_re - probe_im * object_im, probe_re * object_im + probe_im * object_re],
        1,
    ).astype(jnp.bfloat16)
    inner = left_apply(forward, waves).astype(jnp.bfloat16)
    far_turned = left_apply(forward, jnp.swapaxes(inner, 2, 3))
    intensity = jnp.sum(far_turned * far_turned, axis=(0, 1))
    factor = 2.0 * (1.0 - amplitude.T / jnp.sqrt(intensity + 0.5))
    grad_turned = (factor * far_turned).astype(jnp.bfloat16)
    across = left_apply(backward, grad_turned).astype(jnp.bfloat16)
    wave_grad = left_apply(backward, jnp.swapaxes(across, 2, 3))
    grad_re = wave_grad[:, 0]
    grad_im = wave_grad[:, 1]
    object_part = jnp.stack(
        [
            jnp.sum(probe_re * grad_re + probe_im * grad_im, 0),
            jnp.sum(probe_re * grad_im - probe_im * grad_re, 0),
        ],
        0,
    )
    probe_part = jnp.stack(
        [object_re * grad_re + object_im * grad_im, object_re * grad_im - object_im * grad_re], 1
    )
    return (object_part, probe_part)


def add_window(gradient, addend, row_at, col_at):
    anchor = jnp.zeros((), jnp.int32)
    before = lax.dynamic_slice(gradient, (anchor, row_at, col_at), addend.shape)
    return lax.dynamic_update_slice(gradient, before + addend, (anchor, row_at, col_at))


def on_device(object_field, probe, amplitudes, offsets, live):
    extent = probe.shape[2]
    tile_rows = object_field.shape[1]
    tile_cols = object_field.shape[2]
    capacity = offsets.shape[0]
    anchor = jnp.zeros((), jnp.int32)
    right_part = shifted(object_field, "wide", -1)
    rows_block = jnp.concatenate([object_field, right_part], 2)
    below_part = shifted(rows_block[:, :extent, :], "narrow", -1)
    extended = jnp.concatenate([rows_block, below_part], 1)
    local_rows = offsets[:, 0] - lax.axis_index("narrow") * tile_rows
    local_cols = offsets[:, 1] - lax.axis_index("wide") * tile_cols
    count = live[0]
    forward, backward = dft_blocks(extent)

    def own_step(number, carry):
        gradient, probe_sum = carry
        row_at = local_rows[number]
        col_at = local_cols[number]
        window = lax.dynamic_slice(extended, (anchor, row_at, col_at), (2, extent, extent))
        object_part, probe_part = slot_gradients(
            window, probe, amplitudes[number], forward, backward
        )
        return (add_window(gradient, object_part, row_at, col_at), probe_sum + probe_part)

    start = (jnp.zeros(extended.shape, jnp.float32), jnp.zeros(probe.shape, jnp.float32))
    gradient, probe_sum = lax.fori_loop(0, count, own_step, start)
    came_below = shifted(gradient[:, tile_rows:, :], "narrow", 1)
    upper = gradient[:, :tile_rows, :].at[:, :extent, :].add(came_below)
    came_side = shifted(upper[:, :, tile_cols:], "wide", 1)
    object_grad = upper[:, :, :tile_cols].at[:, :, :extent].add(came_side)
    total_slots = lax.axis_size("wide") * lax.axis_size("narrow") * capacity
    probe_grad = lax.psum(probe_sum, ("wide", "narrow")) / math.sqrt(total_slots)
    return (object_grad, probe_grad)


def solution(mesh):
    return jax.shard_map(
        on_device,
        mesh=mesh,
        in_specs=(
            P(None, "narrow", "wide"),
            P(),
            P(("wide", "narrow"), None, None),
            P(("wide", "narrow"), None),
            P(("wide", "narrow")),
        ),
        out_specs=(P(None, "narrow", "wide"), P()),
        check_vma=False,
    )
```

profile of v0, /device:TPU:0, one launch (start us, length us, event | category | flops | bytes accessed | tf_op | source)
XLA Modules:
  0.0 767.0 jit_solution(2804901480739814059)
XLA Ops:
  10.1 26.7 %collective-permute-done = f32[2,512,256]{1,2,0:T(8,128)S(1)} collective-permute-done((f32[2,512,256]{1,2,0:T(8,128)S(1)}, f32[2,512,256]{1,2,0:T(8,128)S(1)}, u32[]{:S(2)}, u32[]{:S(2)}) %collective-permute-start) | collective-permute-done | bytes 1048608 | tf_op jit(solution)/shard_map/ppermute | solution.py:12
  39.2 2.8 copy.17
  45.3 3.1 pad_maximum_fusion.1
  52.3 211.1 %while.15 = (s32[]{:T(128)}, f32[2,768,512]{2,1,0:T(8,128)}, f32[4,2,256,256]{2,1,3,0:T(2,128)}, s32[]{:T(128)}, s32[8]{0:T(128)S(1)}, /*index=5*/s32[8]{0:T(128...) while((s32[]{:T(128)}, f32[2,768,512]{2,1,0:T(8,128)}, ...), condition=%wide.region_5.6_spmd, body=%wide.region_0.5_spmd.sunk | while | flops 2159869952 | bytes 94634512 | solution.py:102
  59.6 2.8 subtract_convert_fusion.2
  66.3 3.1 fusion.43
  70.7 3.8 copy.32
  76.2 4.0 fusion.44
  87.8 3.8 copy.34
  93.3 3.2 convolution_bitcast_fusion.2
  96.5 3.6 reshape.106
  100.1 9.1 %multiply_add_fusion.2 = (f32[4,1,256,256]{2,1,3,0:T(1,128)S(1)}, f32[4,1,256,256]{2,1,3,0:T(1,128)S(1)}, f32[256,256]{0,1:T(8,128)}, f32[256,256]{0,1:T(8,128)}) fusion(f32[256,256]{0,1:T(8,128)S(1)} %copy-done.6, f32[256,256]{0,1:T(8,128)S(1)} %get-tuple-element.236, f32[4,2,256,256]{2,1,3,0:T(2,128)} %reshape.106, ...), kind=kLoop, calls=%fused_computation.12.clone.1 | loop fusion | flops 3538944 | bytes 7340032 | tf_op jit(solution)/shard_map/while/body/add | solution.py:65
  115.8 6.5 dynamic_update_slice.4
  136.2 3.1 fusion.43
  140.6 3.8 copy.32
  146.1 4.0 fusion.44
  157.7 3.8 copy.34
  163.2 3.2 convolution_bitcast_fusion.2
  166.4 3.6 reshape.106
  170.0 9.1 %multiply_add_fusion.2 = (f32[4,1,256,256]{2,1,3,0:T(1,128)S(1)}, f32[4,1,256,256]{2,1,3,0:T(1,128)S(1)}, f32[256,256]{0,1:T(8,128)}, f32[256,256]{0,1:T(8,128)}) fusion(f32[256,256]{0,1:T(8,128)S(1)} %copy-done.6, f32[256,256]{0,1:T(8,128)S(1)} %get-tuple-element.236, f32[4,2,256,256]{2,1,3,0:T(2,128)} %reshape.106, ...), kind=kLoop, calls=%fused_computation.12.clone.1 | loop fusion | flops 3538944 | bytes 7340032 | tf_op jit(solution)/shard_map/while/body/add | solution.py:65
  185.7 6.8 dynamic_update_slice.4
  206.3 3.1 fusion.43
  210.7 3.8 copy.32
  216.2 4.0 fusion.44
  227.8 3.8 copy.34
  233.3 3.2 convolution_bitcast_fusion.2
  236.5 3.6 reshape.106
  240.1 9.1 %multiply_add_fusion.2 = (f32[4,1,256,256]{2,1,3,0:T(1,128)S(1)}, f32[4,1,256,256]{2,1,3,0:T(1,128)S(1)}, f32[256,256]{0,1:T(8,128)}, f32[256,256]{0,1:T(8,128)}) fusion(f32[256,256]{0,1:T(8,128)S(1)} %copy-done.6, f32[256,256]{0,1:T(8,128)S(1)} %get-tuple-element.236, f32[4,2,256,256]{2,1,3,0:T(2,128)} %reshape.106, ...), kind=kLoop, calls=%fused_computation.12.clone.1 | loop fusion | flops 3538944 | bytes 7340032 | tf_op jit(solution)/shard_map/while/body/add | solution.py:65
  255.8 6.7 dynamic_update_slice.4
  273.8 3.8 collective-permute-start.3
  277.6 478.2 %all-reduce.2.cloned.1.call-done = f32[4,2,256,256]{3,2,1,0:T(8,128)} async-done(((f32[4,2,256,256]{3,2,1,0:T(8,128)}), f32[4,2,256,256]{3,2,1,0:T(8,128)}) %all-reduce.2.cloned.1.call-update) | async-done | bytes 2097168 | tf_op jit(solution)/shard_map/psum | solution.py:108
  755.9 3.1 broadcast_multiply_fusion
  (134 shorter events, 105.6 us)
Async XLA Ops:
  7.2 748.7 %all-reduce.2.cloned.1.call-start = ((), (), s32[]{:S(2)}) async-start(), calls=%async_computation | async-start | bytes 4194304 | tf_op jit(solution)/shard_map/psum | solution.py:108
  8.8 28.0 %collective-permute-start = (f32[2,512,256]{1,2,0:T(8,128)S(1)}, f32[2,512,256]{1,2,0:T(8,128)S(1)}, u32[]{:S(2)}, u32[]{:S(2)}) collective-permute-start(f32[2,512,256]{1,2,0:T(8,128)S(1)} %copy.16), channel_id=1, source_target_pairs={{4,0},{8,4},{12,8},{16,12},{20,16},{24,20},{28,24},{5,1},{9,5},{13... | collective-permute-start | bytes 3145736 | tf_op jit(solution)/shard_map/ppermute | solution.py:12
  36.8 2.5 copy-start.8
  37.9 7.4 collective-permute-start.1
  39.2 6.1 copy-start.10
  42.1 3.2 copy-start.9
  59.6 2.8 copy-start.5
  80.2 4.3 copy-start.4
  83.0 1.7 copy-start
  96.5 3.6 copy-start.6
  100.1 9.2 %copy-start.1 = (f32[4,2,256,256]{2,1,3,0:T(2,128)S(1)}, f32[4,2,256,256]{2,1,3,0:T(2,128)}, u32[]{:S(2)}) copy-start(f32[4,2,256,256]{2,1,3,0:T(2,128)} %get-tuple-element.265) | copy-start | bytes 6291460 | tf_op jit(solution)/shard_map/while
  111.7 1.3 copy-start.2
  113.0 1.6 copy-start.7
  129.4 2.8 copy-start.5
  150.1 4.3 copy-start.4
  152.9 1.7 copy-start
  166.3 3.6 copy-start.6
  170.0 9.2 %copy-start.1 = (f32[4,2,256,256]{2,1,3,0:T(2,128)S(1)}, f32[4,2,256,256]{2,1,3,0:T(2,128)}, u32[]{:S(2)}) copy-start(f32[4,2,256,256]{2,1,3,0:T(2,128)} %get-tuple-element.265) | copy-start | bytes 6291460 | tf_op jit(solution)/shard_map/while
  181.5 1.3 copy-start.2
  182.9 1.6 copy-start.7
  199.6 2.8 copy-start.5
  220.2 4.3 copy-start.4
  223.0 1.7 copy-start
  236.5 3.6 copy-start.6
  240.1 9.2 %copy-start.1 = (f32[4,2,256,256]{2,1,3,0:T(2,128)S(1)}, f32[4,2,256,256]{2,1,3,0:T(2,128)}, u32[]{:S(2)}) copy-start(f32[4,2,256,256]{2,1,3,0:T(2,128)} %get-tuple-element.265) | copy-start | bytes 6291460 | tf_op jit(solution)/shard_map/while
  251.7 1.3 copy-start.2
  253.0 1.6 copy-start.7
  263.4 3.8 copy-start.3
  265.8 5.5 collective-permute-start.2
  273.8 485.1 %collective-permute-start.3 = (f32[2,512,256]{2,1,0:T(8,128)}, f32[2,512,256]{2,1,0:T(8,128)S(1)}, u32[]{:S(2)}, u32[]{:S(2)}) collective-permute-start(f32[2,512,256]{2,1,0:T(8,128)} %slice.94), channel_id=1, source_target_pairs={{0,4},{4,8},{8,12},{12,16},{16,20},{20,24},{24,28},{1,5},{5,9},{9,... | collective-permute-start | bytes 3145736 | tf_op jit(solution)/shard_map/ppermute | solution.py:12
Sparse Core Ops, SparseCore 0:
  269.6 486.1 all-reduce.1
where the time goes:
time: 775 us; the launch traced here: 767 us
  waiting for transfers between devices  505 us (65%)
  local copies, waits for them, and re-layouts  115 us (15%)
  other arithmetic  74.2 us (10%)
  matrix products  35.8 us (5%)
  loops' own time  15.2 us (2%)
  between operations  14.2 us (2%)
  starting transfers between devices  7.75 us (1%)
    psum x1, waiting for transfers between devices, on_device(): lax.psum(probe_sum, ('wide', 'narrow')) / math.sqrt(total_slots)  478 us
    dot_general x12, matrix products, left_apply(): jnp.einsum('ab,kbc->kac', block, stacked, preferred_element_type=jnp.floa...  35.8 us
    add x3, other arithmetic, slot_gradients(): object_re * grad_re + object_im * grad_im  27.4 us
    ppermute x4, waiting for transfers between devices, shifted(): lax.ppermute(value, axis, [(source, source + steps) for source in range(f...  26.7 us
    dynamic_update_slice x6, local copies, waits for them, and re-layouts, add_window(): lax.dynamic_update_slice(gradient, before + addend, (anchor, row_at, col_...  20.6 us
  transfers between devices with their start and end apart: 5, of which 2 were waited for; matrix products, arithmetic and copies ran while one was open for 2% of the time, Pallas kernels for 0%

commit v1 on v0

v1 whole, which is shorter than its diff:
```python
import functools
import math

import jax
import jax.numpy as jnp
import ml_dtypes
import numpy as np
from jax import lax
from jax.experimental import pallas as pl
from jax.experimental.pallas import tpu as pltpu
from jax.sharding import PartitionSpec as P

F32 = jnp.float32
BF16 = jnp.bfloat16
LANES = 128


def half_dft(extent):
    half = extent // 2
    blocks = []
    for parity in range(2):
        freq = 2 * np.arange(half)[:, None] + parity
        angles = (freq * np.arange(half)[None, :] % extent) * (2.0 * math.pi / extent)
        cosine = np.cos(angles) / math.sqrt(extent)
        sine = np.sin(angles) / math.sqrt(extent)
        blocks.append(np.block([[cosine, sine], [-sine, cosine]]))
    both = np.stack(blocks)
    return np.stack([both, np.swapaxes(both, 1, 2)]).astype(ml_dtypes.bfloat16)


def parity_order(extent):
    order = np.concatenate([np.arange(0, extent, 2), np.arange(1, extent, 2)])
    matrix = np.zeros((extent, extent), np.float32)
    matrix[order, np.arange(extent)] = 1.0
    return matrix


def dot(a, b):
    return jnp.dot(a, b, preferred_element_type=F32)


def slots_kernel(
    tile_rows, tile_cols, offsets, live, own, below, right, corner, probe, amps, mats,
    grad_own, grad_below, grad_right, grad_corner, probe_sum,
    ext, grad, window, part, amp, waves, inner, far, power, across, in_sems, amp_sems, out_sems,
):
    modes = probe.shape[0]
    extent = probe.shape[2]
    half = extent // 2
    rows_step = 32
    count = live[0]

    pieces = [
        (own, grad_own, slice(0, tile_rows), slice(0, tile_cols)),
        (below, grad_below, slice(tile_rows, tile_rows + extent), slice(0, tile_cols)),
        (right, grad_right, slice(0, tile_rows), slice(tile_cols, tile_cols + extent)),
        (corner, grad_corner, slice(tile_rows, tile_rows + extent), slice(tile_cols, tile_cols + extent)),
    ]
    loads = [
        pltpu.make_async_copy(src, ext.at[:, rows, cols], in_sems.at[n])
        for n, (src, _, rows, cols) in enumerate(pieces)
    ]
    for load in loads:
        load.start()

    def amp_copy(number, place):
        return pltpu.make_async_copy(amps.at[number], amp.at[place], amp_sems.at[place])

    amp_copy(0, 0).start()
    grad[...] = jnp.zeros_like(grad)
    probe_sum[...] = jnp.zeros_like(probe_sum)
    for load in loads:
        load.wait()
    groups = rows_step // 8
    lane = lax.broadcasted_iota(jnp.int32, (rows_step, LANES), 1)
    lane3 = lax.broadcasted_iota(jnp.int32, (groups + 1, 8, LANES), 2)
    sublane = lax.broadcasted_iota(jnp.int32, (groups, 8, LANES), 1)
    sublane_tall = lax.broadcasted_iota(jnp.int32, (groups + 1, 8, LANES), 1)

    @pl.loop(0, count)
    def _(number):
        place = lax.rem(number, 2)

        @pl.when(number + 1 < count)
        def _():
            amp_copy(number + 1, 1 - place).start()

        row_at = lax.rem(offsets[number, 0], tile_rows)
        col_at = lax.rem(offsets[number, 1], tile_cols)
        shift = lax.rem(col_at, LANES)
        col_base = pl.multiple_of(col_at - shift, LANES)
        back = lax.rem(LANES - shift, LANES)
        wide_cols = extent // LANES + 1
        row_shift = lax.rem(row_at, 8)
        row_base = pl.multiple_of(row_at - row_shift, 8)
        row_back = lax.rem(8 - row_shift, 8)

        for plane in range(2):
            for row in range(0, extent, rows_step):
                turned = []
                for c in range(wide_cols):
                    tall = ext[plane, pl.ds(row_base + row, rows_step + 8), pl.ds(col_base + LANES * c, LANES)]
                    tall = pltpu.roll(tall.reshape(groups + 1, 8, LANES), row_back, 1)
                    flat = jnp.where(sublane < 8 - row_shift, tall[:-1], tall[1:]).reshape(rows_step, LANES)
                    turned.append(pltpu.roll(flat, back, 1))
                for c in range(wide_cols - 1):
                    window[plane, row : row + rows_step, c * LANES : (c + 1) * LANES] = jnp.where(
                        lane < LANES - shift, turned[c], turned[c + 1]
                    )

        for k in range(modes):
            for row in range(0, half, rows_step):
                waves_at = []
                for base in (row, half + row):
                    rows = slice(base, base + rows_step)
                    pr, pi = probe[k, 0, rows, :], probe[k, 1, rows, :]
                    o_re, o_im = window[0, rows, :], window[1, rows, :]
                    waves_at.append((pr * o_re - pi * o_im, pr * o_im + pi * o_re))
                for c in range(2):
                    rows = slice(c * half + row, c * half + row + rows_step)
                    waves[k, 0, rows, :] = (waves_at[0][c] + waves_at[1][c]).astype(BF16)
                    waves[k, 1, rows, :] = (waves_at[0][c] - waves_at[1][c]).astype(BF16)
            for a in range(2):
                z = dot(mats[0, a], waves[k, a])
                left, right_half = z[:, :half], z[:, half:]
                for b, value in enumerate((left + right_half, left - right_half)):
                    value = value.astype(BF16)
                    inner[k, b, a * half : (a + 1) * half, :half] = value[:half]
                    inner[k, b, a * half : (a + 1) * half, half:] = value[half:]
            for b in range(2):
                f = dot(inner[k, b], mats[1, b])
                far[k, b] = f
                own_power = f[:, :half] * f[:, :half] + f[:, half:] * f[:, half:]
                power[b] = own_power if k == 0 else power[b] + own_power

        amp_copy(number, place).wait()
        for b in range(2):
            power[b] = 2.0 - 2.0 * amp[place, :, b * half : (b + 1) * half] * lax.rsqrt(power[b] + 0.5)

        for k in range(modes):
            ys = []
            for b in range(2):
                factor = power[b]
                g = jnp.concatenate([far[k, b, :, :half] * factor, far[k, b, :, half:] * factor], 1)
                ys.append(dot(g.astype(BF16), mats[0, b]))
            for side, y in enumerate((ys[0] + ys[1], ys[0] - ys[1])):
                y = y.astype(BF16)
                cols = slice(side * half, (side + 1) * half)
                for a in range(2):
                    rows = slice(a * half, (a + 1) * half)
                    across[k, a, :half, cols] = y[rows, :half]
                    across[k, a, half:, cols] = y[rows, half:]
            v0 = dot(mats[1, 0], across[k, 0])
            v1 = dot(mats[1, 1], across[k, 1])
            for side, v in enumerate((v0 + v1, v0 - v1)):
                rows = slice(side * half, (side + 1) * half)
                g_re, g_im = v[:half], v[half:]
                pr, pi = probe[k, 0, rows, :], probe[k, 1, rows, :]
                o_re, o_im = window[0, rows, :], window[1, rows, :]
                add_re = pr * g_re + pi * g_im
                add_im = pr * g_im - pi * g_re
                part[0, rows, :] = add_re if k == 0 else part[0, rows, :] + add_re
                part[1, rows, :] = add_im if k == 0 else part[1, rows, :] + add_im
                probe_sum[k, 0, rows, :] += o_re * g_re + o_im * g_im
                probe_sum[k, 1, rows, :] += o_re * g_im - o_im * g_re

        zero = jnp.zeros((groups + 1, 8, LANES), F32)
        edge = jnp.zeros((1, 8, LANES), F32)
        for plane in range(2):
            for row in range(0, extent, rows_step):
                turned = []
                for c in range(wide_cols - 1):
                    flat = part[plane, row : row + rows_step, c * LANES : (c + 1) * LANES]
                    flat = pltpu.roll(flat, shift, 1).reshape(groups, 8, LANES)
                    flat = pltpu.roll(flat, row_shift, 1)
                    low = jnp.concatenate([flat, edge], 0)
                    high = jnp.concatenate([edge, flat], 0)
                    turned.append(jnp.where(sublane_tall >= row_shift, low, high))
                turned = [zero] + turned + [zero]
                for c in range(wide_cols):
                    at = (plane, pl.ds(row_base + row, rows_step + 8), pl.ds(col_base + LANES * c, LANES))
                    value = jnp.where(lane3 >= shift, turned[c + 1], turned[c])
                    grad[at] += value.reshape(rows_step + 8, LANES)

    stores = [
        pltpu.make_async_copy(grad.at[:, rows, cols], dst, out_sems.at[n])
        for n, (_, dst, rows, cols) in enumerate(pieces)
    ]
    for store in stores:
        store.start()
    for store in stores:
        store.wait()


def run_slots(offsets, live, own, below, right, corner, probe, amps):
    extent = probe.shape[2]
    modes = probe.shape[0]
    tile_rows, tile_cols = own.shape[1:]
    mats = jnp.asarray(half_dft(extent))
    smem = pl.BlockSpec(memory_space=pltpu.SMEM)
    vmem = pl.BlockSpec(memory_space=pltpu.VMEM)
    hbm = pl.BlockSpec(memory_space=pl.ANY)
    shape = jax.ShapeDtypeStruct
    return pl.pallas_call(
        functools.partial(slots_kernel, tile_rows, tile_cols),
        out_shape=[shape(v.shape, F32) for v in (own, below, right, corner, probe)],
        in_specs=[smem, smem, hbm, hbm, hbm, hbm, vmem, hbm, vmem],
        out_specs=[hbm, hbm, hbm, hbm, vmem],
        scratch_shapes=[
            pltpu.VMEM((2, tile_rows + extent, tile_cols + extent), F32),
            pltpu.VMEM((2, tile_rows + extent, tile_cols + extent), F32),
            pltpu.VMEM((2, extent, extent), F32),
            pltpu.VMEM((2, extent, extent), F32),
            pltpu.VMEM((2, extent, extent), F32),
            pltpu.VMEM((modes, 2, extent, extent), BF16),
            pltpu.VMEM((modes, 2, extent, extent), BF16),
            pltpu.VMEM((modes, 2, extent, extent), F32),
            pltpu.VMEM((2, extent, extent // 2), F32),
            pltpu.VMEM((modes, 2, extent, extent), BF16),
            pltpu.SemaphoreType.DMA((4,)),
            pltpu.SemaphoreType.DMA((2,)),
            pltpu.SemaphoreType.DMA((4,)),
        ],
        compiler_params=pltpu.CompilerParams(vmem_limit_bytes=48 * 1024 * 1024),
        name="slots",
    )(offsets, live, own, below, right, corner, probe, amps, mats)


def shifted(value, axis, steps):
    count = lax.axis_size(axis)
    first, last = (max(0, -steps), min(count, count - steps))
    return lax.ppermute(value, axis, [(source, source + steps) for source in range(first, last)])


def swapped(value, axis, bit):
    count = lax.axis_size(axis)
    return lax.ppermute(value, axis, [(source, source ^ bit) for source in range(count)])


def halve(value, axis, bit):
    upper = (lax.axis_index(axis) & bit) != 0
    low, high = jnp.split(value, 2, 0)
    came = swapped(jnp.where(upper, low, high), axis, bit)
    return jnp.where(upper, high, low) + came


def double(value, axis, bit):
    upper = (lax.axis_index(axis) & bit) != 0
    came = swapped(value, axis, bit)
    return jnp.concatenate([jnp.where(upper, came, value), jnp.where(upper, value, came)], 0)


def sum_everywhere(value):
    narrow = [("narrow", 1 << n) for n in range(lax.axis_size("narrow").bit_length() - 1)]
    wide = [("wide", 1 << n) for n in range(lax.axis_size("wide").bit_length() - 1)]
    first, rest = narrow[0], narrow[1:] + wide
    turning, last = rest[:3], rest[3:]
    value = halve(value, *first)
    unit = value.shape[0] // 8
    parts = jnp.split(value, [3 * unit, 6 * unit], 0)
    orders = [turning[n:] + turning[:n] + last for n in range(3)]
    for step in range(len(rest)):
        parts = [halve(part, *order[step]) for part, order in zip(parts, orders)]
    for step in reversed(range(len(rest))):
        parts = [double(part, *order[step]) for part, order in zip(parts, orders)]
    return double(jnp.concatenate(parts, 0), *first)


def on_device(object_field, probe, amplitudes, offsets, live):
    extent = probe.shape[2]
    order = jnp.asarray(parity_order(extent))
    amps = jnp.einsum("rq,prc,cd->pqd", order, amplitudes, order, precision=lax.Precision.HIGHEST)
    right = shifted(object_field[:, :, :extent], "wide", -1)
    below = shifted(object_field[:, :extent, :], "narrow", -1)
    corner = shifted(right[:, :extent, :], "narrow", -1)
    grad_own, grad_below, grad_right, grad_corner, probe_sum = run_slots(
        offsets, live, object_field, below, right, corner, probe, amps
    )
    total_slots = lax.axis_size("wide") * lax.axis_size("narrow") * offsets.shape[0]
    scaled = (probe_sum / math.sqrt(total_slots)).reshape(-1, extent)
    probe_grad = sum_everywhere(scaled).reshape(probe.shape)
    came_below = shifted(grad_below, "narrow", 1)
    came_corner = shifted(grad_corner, "narrow", 1)
    came_right = shifted(grad_right.at[:, :extent, :].add(came_corner), "wide", 1)
    object_grad = grad_own.at[:, :extent, :].add(came_below).at[:, :, :extent].add(came_right)
    return (object_grad, probe_grad)


def solution(mesh):
    return jax.shard_map(
        on_device,
        mesh=mesh,
        in_specs=(
            P(None, "narrow", "wide"),
            P(),
            P(("wide", "narrow"), None, None),
            P(("wide", "narrow"), None),
            P(("wide", "narrow")),
        ),
        out_specs=(P(None, "narrow", "wide"), P()),
        check_vma=False,
    )
```

time: 775 us -> 182 us (0.23)
  the two profiles are of different devices: /device:TPU:0 before, /device:TPU:1 now
where the time goes in v1:
time: 182 us; the launch traced here: 181 us
  waiting for transfers between devices  75.9 us (42%)
  starting transfers between devices  69.9 us (38%)
  other arithmetic  12.1 us (7%)
  Pallas kernels  9.26 us (5%)
  local copies, waits for them, and re-layouts  6.56 us (4%)
  matrix products  5.01 us (3%)
  between operations  1.84 us (1%)
    ppermute x26, starting transfers between devices, swapped(): lax.ppermute(value, axis, [(source, source ^ bit) for source in range(cou...  51.4 us
    ppermute x26, waiting for transfers between devices, swapped(): lax.ppermute(value, axis, [(source, source ^ bit) for source in range(cou...  41.9 us
    ppermute x6, waiting for transfers between devices, shifted(): lax.ppermute(value, axis, [(source, source + steps) for source in range(f...  34 us
    ppermute x6, starting transfers between devices, shifted(): lax.ppermute(value, axis, [(source, source + steps) for source in range(f...  18.5 us
    pallas_call x1, Pallas kernels, run_slots(): pl.pallas_call(functools.partial(slots_kernel, tile_rows, tile_cols), out...  9.26 us
    dot_general x2, matrix products, on_device(): jnp.einsum('rq,prc,cd->pqd', order, amplitudes, order, precision=lax.Prec...  5.01 us
  transfers between devices with their start and end apart: 32, of which 20 were waited for; matrix products, arithmetic and copies ran while one was open for 8% of the time, Pallas kernels for 0%

profile of v1, /device:TPU:1, one launch (start us, length us, event | category | flops | bytes accessed | tf_op | source)
XLA Modules:
  0.0 180.6 jit_solution(7859799558419934988)
XLA Ops:
  2.1 1.9 %slice.81 = f32[2,256,256]{2,1,0:T(8,128)} slice(f32[2,512,256]{2,1,0:T(8,128)} %own.1), slice={[0:2], [0:256], [0:256]} | slice | bytes 1048576 | tf_op jit(solution)/shard_map/slice | solution.py:274
  4.0 2.0 %collective-permute-start = (f32[2,256,256]{2,1,0:T(8,128)}, f32[2,256,256]{2,1,0:T(8,128)S(1)}, u32[]{:S(2)}, u32[]{:S(2)}) collective-permute-start(f32[2,256,256]{2,1,0:T(8,128)} %slice.81), channel_id=1, source_target_pairs={{1,0},{2,1},{3,2},{5,4},{6,5},{7,6},{9,8},{10,9},{11,10},{13,12},{... | collective-permute-start | bytes 1572872 | tf_op jit(solution)/shard_map/ppermute | solution.py:232
  7.3 20.6 %collective-permute-done.1.right = f32[2,512,256]{2,1,0:T(8,128)} collective-permute-done((f32[2,512,256]{2,1,0:T(8,128)}, f32[2,512,256]{2,1,0:T(8,128)}, u32[]{:S(2)}, u32[]{:S(2)}) %collective-permute-start.1) | collective-permute-done | bytes 1048608 | tf_op jit(solution)/shard_map/ppermute | solution.py:232
  29.0 3.1 %collective-permute-start.2 = (f32[2,256,256]{2,1,0:T(8,128)S(1)}, f32[2,256,256]{2,1,0:T(8,128)S(1)}, u32[]{:S(2)}, u32[]{:S(2)}) collective-permute-start(f32[2,256,256]{2,1,0:T(8,128)S(1)} %slice.85), channel_id=1, source_target_pairs={{1,0},{2,1},{3,2},{5,4},{6,5},{7,6},{9,8},{10,9},{11,10},{13,12},{... | collective-permute-start | bytes 1572872 | tf_op jit(solution)/shard_map/ppermute | solution.py:232
  32.2 1.9 %fusion.2 = f32[256,8,256]{2,0,1:T(8,128)S(1)} fusion(f32[256,256,1]{1,0,2:T(8,128)S(1)} %copy-done.10, f32[8,256,256]{2,1,0:T(8,128)S(1)} %copy-done), kind=kOutput, calls=%fused_computation.68 | convolution fusion | flops 1610612736 | bytes 4456448 | tf_op jit(solution)/shard_map/rq,prc,cd->pqd/dot_general | solution.py:272
  34.1 3.1 %fusion.amps = f32[8,256,256]{2,1,0:T(8,128)} fusion(f32[256,256,1]{1,0,2:T(8,128)S(1)} %copy-done.10, f32[256,8,256]{2,0,1:T(8,128)S(1)} %fusion.2), kind=kOutput, calls=%fused_computation.1 | convolution fusion | flops 1610612736 | bytes 4456448 | tf_op jit(solution)/shard_map/rq,prc,cd->pqd/dot_general | solution.py:272
  38.0 2.4 %collective-permute-done.2.corner = f32[2,256,256]{2,1,0:T(8,128)S(1)} collective-permute-done((f32[2,256,256]{2,1,0:T(8,128)S(1)}, f32[2,256,256]{2,1,0:T(8,128)S(1)}, u32[]{:S(2)}, u32[]{:S(2)}) %collective-permute-start.2) | collective-permute-done | bytes 524320 | tf_op jit(solution)/shard_map/ppermute | solution.py:232
  41.4 9.3 %slots.1 = (f32[2,512,256]{2,1,0:T(8,128)S(1)}, f32[2,256,256]{2,1,0:T(8,128)S(1)}, f32[2,512,256]{2,1,0:T(8,128)S(1)}, f32[2,256,256]{2,1,0:T(8,128)}, f32[4,2,256,256]{3,2,1,0:T(8,128)}) custom-call(s32[8,2]{1,0:T(8,128)S(1)} %copy.9.offsets, s32[1]{0:T(128)S(6)} %copy.17.live, f32[2,512,256]{2,1,0:T(8,128)S(1)} %copy-done.1, ...), custom_call_target="tpu_custom_call" | custom-call | tf_op jit(solution)/shard_map/slots/pallas_call | solution.py:204
  50.7 2.3 %broadcast_multiply_fusion = f32[4,2,256,256]{3,2,1,0:T(8,128)S(1)} fusion(f32[4,2,256,256]{3,2,1,0:T(8,128)} %get-tuple-element.55), kind=kLoop, calls=%fused_computation.4 | loop fusion | flops 524288 | bytes 4194304 | tf_op jit(solution)/shard_map/div | solution.py:280
  55.2 2.6 %collective-permute-done.6 = f32[1024,256]{1,0:T(8,128)} collective-permute-done((f32[1024,256]{1,0:T(8,128)}, f32[1024,256]{1,0:T(8,128)}, u32[]{:S(2)}, u32[]{:S(2)}) %collective-permute-start.6) | collective-permute-done | bytes 1048608 | tf_op jit(solution)/shard_map/ppermute | solution.py:237
  57.8 1.7 bitcast_add_fusion
  60.5 8.8 %collective-permute-start.23 = (f32[128,256]{1,0:T(8,128)S(1)}, f32[128,256]{1,0:T(8,128)S(1)}, u32[]{:S(2)}, u32[]{:S(2)}) collective-permute-start(f32[128,256]{1,0:T(8,128)S(1)} %slice_select_fusion.4), channel_id=1, source_target_pairs={{0,8},{4,12},{8,0},{12,4},{16,24},{20,28},{24,16},{28,20},{1,9},{5... | collective-permute-start | bytes 393224 | tf_op jit(solution)/shard_map/ppermute | solution.py:237
  69.3 5.1 %collective-permute-start.4 = (f32[2,256,256]{2,1,0:T(8,128)}, f32[2,256,256]{2,1,0:T(8,128)}, u32[]{:S(2)}, u32[]{:S(2)}) collective-permute-start(f32[2,256,256]{2,1,0:T(8,128)} %get-tuple-element.54), channel_id=1, source_target_pairs={{0,1},{1,2},{2,3},{4,5},{5,6},{6,7},{8,9},{9,10},{10,11},{12,13},{... | collective-permute-start | bytes 1572872 | tf_op jit(solution)/shard_map/ppermute | solution.py:232
  76.7 4.9 %collective-permute-done.4 = f32[2,256,256]{2,1,0:T(8,128)} collective-permute-done((f32[2,256,256]{2,1,0:T(8,128)}, f32[2,256,256]{2,1,0:T(8,128)}, u32[]{:S(2)}, u32[]{:S(2)}) %collective-permute-start.4) | collective-permute-done | bytes 524320 | tf_op jit(solution)/shard_map/ppermute | solution.py:232
  81.6 2.1 %add_dynamic-update-slice_fusion = f32[2,512,256]{2,1,0:T(8,128)} fusion(f32[2,512,256]{2,1,0:T(8,128)} %copy-done.5, f32[2,256,256]{2,1,0:T(8,128)} %collective-permute-done.4), kind=kLoop, calls=%fused_computation.7 | loop fusion | flops 131072 | bytes 1572864 | tf_op jit(solution)/shard_map/scatter-add | solution.py:284
  83.7 4.1 %collective-permute-start.5 = (f32[2,512,256]{2,1,0:T(8,128)}, f32[2,512,256]{2,1,0:T(8,128)S(1)}, u32[]{:S(2)}, u32[]{:S(2)}) collective-permute-start(f32[2,512,256]{2,1,0:T(8,128)} %add_dynamic-update-slice_fusion), channel_id=1, source_target_pairs={{0,4},{4,8},{8,12},{12,16},{16,20},{20,24},{24,28},{1,5},{5,9},{9,... | collective-permute-start | bytes 3145736 | tf_op jit(solution)/shard_map/ppermute | solution.py:232
  89.5 21.0 %collective-permute-done.25 = f32[32,256]{1,0:T(8,128)S(1)} collective-permute-done((f32[32,256]{1,0:T(8,128)S(1)}, f32[32,256]{1,0:T(8,128)S(1)}, u32[]{:S(2)}, u32[]{:S(2)}) %collective-permute-start.25) | collective-permute-done | bytes 32800 | tf_op jit(solution)/shard_map/ppermute | solution.py:237
  110.5 13.8 %collective-permute-start.26 = (f32[16,256]{1,0:T(8,128)S(1)}, f32[16,256]{1,0:T(8,128)S(1)}, u32[]{:S(2)}, u32[]{:S(2)}) collective-permute-start(f32[16,256]{1,0:T(8,128)S(1)} %slice_select_fusion.13), channel_id=1, source_target_pairs={{0,16},{4,20},{8,24},{12,28},{16,0},{20,4},{24,8},{28,12},{1,17},{... | collective-permute-start | bytes 49160 | tf_op jit(solution)/shard_map/ppermute | solution.py:237
  125.7 2.5 %collective-permute-start.27 = (f32[16,256]{1,0:T(8,128)S(1)}, f32[16,256]{1,0:T(8,128)S(1)}, u32[]{:S(2)}, u32[]{:S(2)}) collective-permute-start(f32[16,256]{1,0:T(8,128)S(1)} %select_add_fusion.11), channel_id=1, source_target_pairs={{0,16},{4,20},{8,24},{12,28},{16,0},{20,4},{24,8},{28,12},{1,17},{... | collective-permute-start | bytes 49160 | tf_op jit(solution)/shard_map/ppermute | solution.py:237
  129.6 1.9 %collective-permute-start.28 = (f32[32,256]{1,0:T(8,128)S(1)}, f32[32,256]{1,0:T(8,128)S(1)}, u32[]{:S(2)}, u32[]{:S(2)}) collective-permute-start(f32[32,256]{1,0:T(8,128)S(1)} %pad_maximum_fusion.9), channel_id=1, source_target_pairs={{0,4},{4,0},{8,12},{12,8},{16,20},{20,16},{24,28},{28,24},{1,5},{5... | collective-permute-start | bytes 98312 | tf_op jit(solution)/shard_map/ppermute | solution.py:237
  131.6 1.8 %collective-permute-done.28 = f32[32,256]{1,0:T(8,128)S(1)} collective-permute-done((f32[32,256]{1,0:T(8,128)S(1)}, f32[32,256]{1,0:T(8,128)S(1)}, u32[]{:S(2)}, u32[]{:S(2)}) %collective-permute-start.28) | collective-permute-done | bytes 32800 | tf_op jit(solution)/shard_map/ppermute | solution.py:237
  137.8 2.1 %collective-permute-start.18 = (f32[24,256]{1,0:T(8,128)S(1)}, f32[24,256]{1,0:T(8,128)S(1)}, u32[]{:S(2)}, u32[]{:S(2)}) collective-permute-start(f32[24,256]{1,0:T(8,128)S(1)} %slice_select_fusion.11), channel_id=1, source_target_pairs={{0,16},{4,20},{8,24},{12,28},{16,0},{20,4},{24,8},{28,12},{1,17},{... | collective-permute-start | bytes 73736 | tf_op jit(solution)/shard_map/ppermute | solution.py:237
  140.5 1.8 %collective-permute-start.30 = (f32[128,256]{1,0:T(8,128)S(1)}, f32[128,256]{1,0:T(8,128)S(1)}, u32[]{:S(2)}, u32[]{:S(2)}) collective-permute-start(f32[128,256]{1,0:T(8,128)S(1)} %pad_maximum_fusion.3), channel_id=1, source_target_pairs={{0,8},{4,12},{8,0},{12,4},{16,24},{20,28},{24,16},{28,20},{1,9},{5... | collective-permute-start | bytes 393224 | tf_op jit(solution)/shard_map/ppermute | solution.py:237
  142.3 1.7 collective-permute-done.10
  144.1 2.4 %collective-permute-start.19 = (f32[24,256]{1,0:T(8,128)S(1)}, f32[24,256]{1,0:T(8,128)S(1)}, u32[]{:S(2)}, u32[]{:S(2)}) collective-permute-start(f32[24,256]{1,0:T(8,128)S(1)} %select_add_fusion.9), channel_id=1, source_target_pairs={{0,16},{4,20},{8,24},{12,28},{16,0},{20,4},{24,8},{28,12},{1,17},{... | collective-permute-start | bytes 73736 | tf_op jit(solution)/shard_map/ppermute | solution.py:237
  148.7 2.0 %collective-permute-done.12 = f32[48,256]{1,0:T(8,128)S(1)} collective-permute-done((f32[48,256]{1,0:T(8,128)S(1)}, f32[48,256]{1,0:T(8,128)S(1)}, u32[]{:S(2)}, u32[]{:S(2)}) %collective-permute-start.12) | collective-permute-done | bytes 49184 | tf_op jit(solution)/shard_map/ppermute | solution.py:237
  152.7 1.6 collective-permute-done.13
  156.0 3.0 %collective-permute-done.14 = f32[192,256]{1,0:T(8,128)S(1)} collective-permute-done((f32[192,256]{1,0:T(8,128)S(1)}, f32[192,256]{1,0:T(8,128)S(1)}, u32[]{:S(2)}, u32[]{:S(2)}) %collective-permute-start.14) | collective-permute-done | bytes 196640 | tf_op jit(solution)/shard_map/ppermute | solution.py:237
  159.0 1.8 %collective-permute-done.22 = f32[192,256]{1,0:T(8,128)S(1)} collective-permute-done((f32[192,256]{1,0:T(8,128)S(1)}, f32[192,256]{1,0:T(8,128)S(1)}, u32[]{:S(2)}, u32[]{:S(2)}) %collective-permute-start.22) | collective-permute-done | bytes 196640 | tf_op jit(solution)/shard_map/ppermute | solution.py:237
  161.0 7.9 %collective-permute-start.31 = (f32[1024,256]{1,0:T(8,128)S(1)}, f32[1024,256]{1,0:T(8,128)S(1)}, u32[]{:S(2)}, u32[]{:S(2)}) collective-permute-start(f32[1024,256]{1,0:T(8,128)S(1)} %select_dynamic-update-slice_fusion.4), channel_id=1, source_target_pairs={{0,1},{1,0},{2,3},{3,2},{4,5},{5,4},{6,7},{7,6},{8,9},{9,8},{10,11... | collective-permute-start | bytes 3145736 | tf_op jit(solution)/shard_map/ppermute | solution.py:237
  168.9 2.7 %collective-permute-start.3 = (f32[2,256,256]{2,1,0:T(8,128)S(1)}, f32[2,256,256]{2,1,0:T(8,128)S(1)}, u32[]{:S(2)}, u32[]{:S(2)}) collective-permute-start(f32[2,256,256]{2,1,0:T(8,128)S(1)} %copy-done.7), channel_id=1, source_target_pairs={{0,1},{1,2},{2,3},{4,5},{5,6},{6,7},{8,9},{9,10},{10,11},{12,13},{... | collective-permute-start | bytes 1572872 | tf_op jit(solution)/shard_map/ppermute | solution.py:232
  171.6 6.1 %collective-permute-done.3 = f32[2,256,256]{2,1,0:T(8,128)S(1)} collective-permute-done((f32[2,256,256]{2,1,0:T(8,128)S(1)}, f32[2,256,256]{2,1,0:T(8,128)S(1)}, u32[]{:S(2)}, u32[]{:S(2)}) %collective-permute-start.3) | collective-permute-done | bytes 524320 | tf_op jit(solution)/shard_map/ppermute | solution.py:232
  (114 shorter events, 28.6 us)
Async XLA Ops:
  0.7 27.3 %collective-permute-start.1 = (f32[2,512,256]{2,1,0:T(8,128)}, f32[2,512,256]{2,1,0:T(8,128)}, u32[]{:S(2)}, u32[]{:S(2)}) collective-permute-start(f32[2,512,256]{2,1,0:T(8,128)} %own.1), channel_id=1, source_target_pairs={{4,0},{8,4},{12,8},{16,12},{20,16},{24,20},{28,24},{5,1},{9,5},{13... | collective-permute-start | bytes 3145736 | tf_op jit(solution)/shard_map/ppermute | solution.py:232
  4.0 33.3 %collective-permute-start = (f32[2,256,256]{2,1,0:T(8,128)}, f32[2,256,256]{2,1,0:T(8,128)S(1)}, u32[]{:S(2)}, u32[]{:S(2)}) collective-permute-start(f32[2,256,256]{2,1,0:T(8,128)} %slice.81), channel_id=1, source_target_pairs={{1,0},{2,1},{3,2},{5,4},{6,5},{7,6},{9,8},{10,9},{11,10},{13,12},{... | collective-permute-start | bytes 1572872 | tf_op jit(solution)/shard_map/ppermute | solution.py:232
  29.0 11.4 %collective-permute-start.2 = (f32[2,256,256]{2,1,0:T(8,128)S(1)}, f32[2,256,256]{2,1,0:T(8,128)S(1)}, u32[]{:S(2)}, u32[]{:S(2)}) collective-permute-start(f32[2,256,256]{2,1,0:T(8,128)S(1)} %slice.85), channel_id=1, source_target_pairs={{1,0},{2,1},{3,2},{5,4},{6,5},{7,6},{9,8},{10,9},{11,10},{13,12},{... | collective-permute-start | bytes 1572872 | tf_op jit(solution)/shard_map/ppermute | solution.py:232
  54.6 3.3 %collective-permute-start.6 = (f32[1024,256]{1,0:T(8,128)}, f32[1024,256]{1,0:T(8,128)}, u32[]{:S(2)}, u32[]{:S(2)}) collective-permute-start(f32[1024,256]{1,0:T(8,128)} %bitcast.3), channel_id=1, source_target_pairs={{0,1},{1,0},{2,3},{3,2},{4,5},{5,4},{6,7},{7,6},{8,9},{9,8},{10,11... | collective-permute-start | bytes 3145736 | tf_op jit(solution)/shard_map/ppermute | solution.py:237
  60.5 14.0 %collective-permute-start.23 = (f32[128,256]{1,0:T(8,128)S(1)}, f32[128,256]{1,0:T(8,128)S(1)}, u32[]{:S(2)}, u32[]{:S(2)}) collective-permute-start(f32[128,256]{1,0:T(8,128)S(1)} %slice_select_fusion.4), channel_id=1, source_target_pairs={{0,8},{4,12},{8,0},{12,4},{16,24},{20,28},{24,16},{28,20},{1,9},{5... | collective-permute-start | bytes 393224 | tf_op jit(solution)/shard_map/ppermute | solution.py:237
  69.3 12.3 %collective-permute-start.4 = (f32[2,256,256]{2,1,0:T(8,128)}, f32[2,256,256]{2,1,0:T(8,128)}, u32[]{:S(2)}, u32[]{:S(2)}) collective-permute-start(f32[2,256,256]{2,1,0:T(8,128)} %get-tuple-element.54), channel_id=1, source_target_pairs={{0,1},{1,2},{2,3},{4,5},{5,6},{6,7},{8,9},{9,10},{10,11},{12,13},{... | collective-permute-start | bytes 1572872 | tf_op jit(solution)/shard_map/ppermute | solution.py:232
  75.6 12.2 %collective-permute-start.24 = (f32[64,256]{1,0:T(8,128)S(1)}, f32[64,256]{1,0:T(8,128)S(1)}, u32[]{:S(2)}, u32[]{:S(2)}) collective-permute-start(f32[64,256]{1,0:T(8,128)S(1)} %slice_select_fusion.7), channel_id=1, source_target_pairs={{0,2},{1,3},{2,0},{3,1},{4,6},{5,7},{6,4},{7,5},{8,10},{9,11},{10,... | collective-permute-start | bytes 196616 | tf_op jit(solution)/shard_map/ppermute | solution.py:237
  83.7 94.2 %collective-permute-start.5 = (f32[2,512,256]{2,1,0:T(8,128)}, f32[2,512,256]{2,1,0:T(8,128)S(1)}, u32[]{:S(2)}, u32[]{:S(2)}) collective-permute-start(f32[2,512,256]{2,1,0:T(8,128)} %add_dynamic-update-slice_fusion), channel_id=1, source_target_pairs={{0,4},{4,8},{8,12},{12,16},{16,20},{20,24},{24,28},{1,5},{5,9},{9,... | collective-permute-start | bytes 3145736 | tf_op jit(solution)/shard_map/ppermute | solution.py:232
  87.8 22.7 %collective-permute-start.25 = (f32[32,256]{1,0:T(8,128)S(1)}, f32[32,256]{1,0:T(8,128)S(1)}, u32[]{:S(2)}, u32[]{:S(2)}) collective-permute-start(f32[32,256]{1,0:T(8,128)S(1)} %slice_select_fusion.10), channel_id=1, source_target_pairs={{0,4},{4,0},{8,12},{12,8},{16,20},{20,16},{24,28},{28,24},{1,5},{5... | collective-permute-start | bytes 98312 | tf_op jit(solution)/shard_map/ppermute | solution.py:237
  88.0 36.3 %collective-permute-start.15 = (f32[192,256]{1,0:T(8,128)S(1)}, f32[192,256]{1,0:T(8,128)S(1)}, u32[]{:S(2)}, u32[]{:S(2)}) collective-permute-start(f32[192,256]{1,0:T(8,128)S(1)} %get-tuple-element.62), channel_id=1, source_target_pairs={{0,4},{4,0},{8,12},{12,8},{16,20},{20,16},{24,28},{28,24},{1,5},{5... | collective-permute-start | bytes 589832 | tf_op jit(solution)/shard_map/ppermute | solution.py:237
  89.5 34.8 %collective-permute-start.7 = (f32[192,256]{1,0:T(8,128)S(1)}, f32[192,256]{1,0:T(8,128)S(1)}, u32[]{:S(2)}, u32[]{:S(2)}) collective-permute-start(f32[192,256]{1,0:T(8,128)S(1)} %get-tuple-element.63), channel_id=1, source_target_pairs={{0,2},{1,3},{2,0},{3,1},{4,6},{5,7},{6,4},{7,5},{8,10},{9,11},{10,... | collective-permute-start | bytes 589832 | tf_op jit(solution)/shard_map/ppermute | solution.py:237
  110.5 15.2 %collective-permute-start.26 = (f32[16,256]{1,0:T(8,128)S(1)}, f32[16,256]{1,0:T(8,128)S(1)}, u32[]{:S(2)}, u32[]{:S(2)}) collective-permute-start(f32[16,256]{1,0:T(8,128)S(1)} %slice_select_fusion.13), channel_id=1, source_target_pairs={{0,16},{4,20},{8,24},{12,28},{16,0},{20,4},{24,8},{28,12},{1,17},{... | collective-permute-start | bytes 49160 | tf_op jit(solution)/shard_map/ppermute | solution.py:237
  125.7 3.8 %collective-permute-start.27 = (f32[16,256]{1,0:T(8,128)S(1)}, f32[16,256]{1,0:T(8,128)S(1)}, u32[]{:S(2)}, u32[]{:S(2)}) collective-permute-start(f32[16,256]{1,0:T(8,128)S(1)} %select_add_fusion.11), channel_id=1, source_target_pairs={{0,16},{4,20},{8,24},{12,28},{16,0},{20,4},{24,8},{28,12},{1,17},{... | collective-permute-start | bytes 49160 | tf_op jit(solution)/shard_map/ppermute | solution.py:237
  128.3 5.2 %collective-permute-start.16 = (f32[96,256]{1,0:T(8,128)S(1)}, f32[96,256]{1,0:T(8,128)S(1)}, u32[]{:S(2)}, u32[]{:S(2)}) collective-permute-start(f32[96,256]{1,0:T(8,128)S(1)} %slice_select_fusion.5), channel_id=1, source_target_pairs={{0,8},{4,12},{8,0},{12,4},{16,24},{20,28},{24,16},{28,20},{1,9},{5... | collective-permute-start | bytes 294920 | tf_op jit(solution)/shard_map/ppermute | solution.py:237
  129.6 3.8 %collective-permute-start.28 = (f32[32,256]{1,0:T(8,128)S(1)}, f32[32,256]{1,0:T(8,128)S(1)}, u32[]{:S(2)}, u32[]{:S(2)}) collective-permute-start(f32[32,256]{1,0:T(8,128)S(1)} %pad_maximum_fusion.9), channel_id=1, source_target_pairs={{0,4},{4,0},{8,12},{12,8},{16,20},{20,16},{24,28},{28,24},{1,5},{5... | collective-permute-start | bytes 98312 | tf_op jit(solution)/shard_map/ppermute | solution.py:237
  131.5 4.1 %collective-permute-start.8 = (f32[96,256]{1,0:T(8,128)S(1)}, f32[96,256]{1,0:T(8,128)S(1)}, u32[]{:S(2)}, u32[]{:S(2)}) collective-permute-start(f32[96,256]{1,0:T(8,128)S(1)} %slice_select_fusion.6), channel_id=1, source_target_pairs={{0,4},{4,0},{8,12},{12,8},{16,20},{20,16},{24,28},{28,24},{1,5},{5... | collective-permute-start | bytes 294920 | tf_op jit(solution)/shard_map/ppermute | solution.py:237
  133.4 7.0 %collective-permute-start.29 = (f32[64,256]{1,0:T(8,128)S(1)}, f32[64,256]{1,0:T(8,128)S(1)}, u32[]{:S(2)}, u32[]{:S(2)}) collective-permute-start(f32[64,256]{1,0:T(8,128)S(1)} %pad_maximum_fusion.6), channel_id=1, source_target_pairs={{0,2},{1,3},{2,0},{3,1},{4,6},{5,7},{6,4},{7,5},{8,10},{9,11},{10,... | collective-permute-start | bytes 196616 | tf_op jit(solution)/shard_map/ppermute | solution.py:237
  133.6 4.3 %collective-permute-start.17 = (f32[48,256]{1,0:T(8,128)S(1)}, f32[48,256]{1,0:T(8,128)S(1)}, u32[]{:S(2)}, u32[]{:S(2)}) collective-permute-start(f32[48,256]{1,0:T(8,128)S(1)} %slice_select_fusion.8), channel_id=1, source_target_pairs={{0,2},{1,3},{2,0},{3,1},{4,6},{5,7},{6,4},{7,5},{8,10},{9,11},{10,... | collective-permute-start | bytes 147464 | tf_op jit(solution)/shard_map/ppermute | solution.py:237
  135.6 4.3 %collective-permute-start.9 = (f32[48,256]{1,0:T(8,128)S(1)}, f32[48,256]{1,0:T(8,128)S(1)}, u32[]{:S(2)}, u32[]{:S(2)}) collective-permute-start(f32[48,256]{1,0:T(8,128)S(1)} %slice_select_fusion.9), channel_id=1, source_target_pairs={{0,8},{4,12},{8,0},{12,4},{16,24},{20,28},{24,16},{28,20},{1,9},{5... | collective-permute-start | bytes 147464 | tf_op jit(solution)/shard_map/ppermute | solution.py:237
  137.8 6.2 %collective-permute-start.18 = (f32[24,256]{1,0:T(8,128)S(1)}, f32[24,256]{1,0:T(8,128)S(1)}, u32[]{:S(2)}, u32[]{:S(2)}) collective-permute-start(f32[24,256]{1,0:T(8,128)S(1)} %slice_select_fusion.11), channel_id=1, source_target_pairs={{0,16},{4,20},{8,24},{12,28},{16,0},{20,4},{24,8},{28,12},{1,17},{... | collective-permute-start | bytes 73736 | tf_op jit(solution)/shard_map/ppermute | solution.py:237
  140.0 4.1 %collective-permute-start.10 = (f32[24,256]{1,0:T(8,128)S(1)}, f32[24,256]{1,0:T(8,128)S(1)}, u32[]{:S(2)}, u32[]{:S(2)}) collective-permute-start(f32[24,256]{1,0:T(8,128)S(1)} %slice_select_fusion.12), channel_id=1, source_target_pairs={{0,16},{4,20},{8,24},{12,28},{16,0},{20,4},{24,8},{28,12},{1,17},{... | collective-permute-start | bytes 73736 | tf_op jit(solution)/shard_map/ppermute | solution.py:237
  140.5 20.4 %collective-permute-start.30 = (f32[128,256]{1,0:T(8,128)S(1)}, f32[128,256]{1,0:T(8,128)S(1)}, u32[]{:S(2)}, u32[]{:S(2)}) collective-permute-start(f32[128,256]{1,0:T(8,128)S(1)} %pad_maximum_fusion.3), channel_id=1, source_target_pairs={{0,8},{4,12},{8,0},{12,4},{16,24},{20,28},{24,16},{28,20},{1,9},{5... | collective-permute-start | bytes 393224 | tf_op jit(solution)/shard_map/ppermute | solution.py:237
  144.1 3.7 %collective-permute-start.11 = (f32[24,256]{1,0:T(8,128)S(1)}, f32[24,256]{1,0:T(8,128)S(1)}, u32[]{:S(2)}, u32[]{:S(2)}) collective-permute-start(f32[24,256]{1,0:T(8,128)S(1)} %select_add_fusion.10), channel_id=1, source_target_pairs={{0,16},{4,20},{8,24},{12,28},{16,0},{20,4},{24,8},{28,12},{1,17},{... | collective-permute-start | bytes 73736 | tf_op jit(solution)/shard_map/ppermute | solution.py:237
  144.1 3.9 %collective-permute-start.19 = (f32[24,256]{1,0:T(8,128)S(1)}, f32[24,256]{1,0:T(8,128)S(1)}, u32[]{:S(2)}, u32[]{:S(2)}) collective-permute-start(f32[24,256]{1,0:T(8,128)S(1)} %select_add_fusion.9), channel_id=1, source_target_pairs={{0,16},{4,20},{8,24},{12,28},{16,0},{20,4},{24,8},{28,12},{1,17},{... | collective-permute-start | bytes 73736 | tf_op jit(solution)/shard_map/ppermute | solution.py:237
  147.7 3.0 %collective-permute-start.12 = (f32[48,256]{1,0:T(8,128)S(1)}, f32[48,256]{1,0:T(8,128)S(1)}, u32[]{:S(2)}, u32[]{:S(2)}) collective-permute-start(f32[48,256]{1,0:T(8,128)S(1)} %pad_maximum_fusion.7), channel_id=1, source_target_pairs={{0,8},{4,12},{8,0},{12,4},{16,24},{20,28},{24,16},{28,20},{1,9},{5... | collective-permute-start | bytes 147464 | tf_op jit(solution)/shard_map/ppermute | solution.py:237
  148.0 3.3 %collective-permute-start.20 = (f32[48,256]{1,0:T(8,128)S(1)}, f32[48,256]{1,0:T(8,128)S(1)}, u32[]{:S(2)}, u32[]{:S(2)}) collective-permute-start(f32[48,256]{1,0:T(8,128)S(1)} %pad_maximum_fusion.8), channel_id=1, source_target_pairs={{0,2},{1,3},{2,0},{3,1},{4,6},{5,7},{6,4},{7,5},{8,10},{9,11},{10,... | collective-permute-start | bytes 147464 | tf_op jit(solution)/shard_map/ppermute | solution.py:237
  150.8 3.5 %collective-permute-start.13 = (f32[96,256]{1,0:T(8,128)S(1)}, f32[96,256]{1,0:T(8,128)S(1)}, u32[]{:S(2)}, u32[]{:S(2)}) collective-permute-start(f32[96,256]{1,0:T(8,128)S(1)} %pad_maximum_fusion.4), channel_id=1, source_target_pairs={{0,4},{4,0},{8,12},{12,8},{16,20},{20,16},{24,28},{28,24},{1,5},{5... | collective-permute-start | bytes 294920 | tf_op jit(solution)/shard_map/ppermute | solution.py:237
  151.3 3.8 %collective-permute-start.21 = (f32[96,256]{1,0:T(8,128)S(1)}, f32[96,256]{1,0:T(8,128)S(1)}, u32[]{:S(2)}, u32[]{:S(2)}) collective-permute-start(f32[96,256]{1,0:T(8,128)S(1)} %pad_maximum_fusion.5), channel_id=1, source_target_pairs={{0,8},{4,12},{8,0},{12,4},{16,24},{20,28},{24,16},{28,20},{1,9},{5... | collective-permute-start | bytes 294920 | tf_op jit(solution)/shard_map/ppermute | solution.py:237
  154.4 4.6 %collective-permute-start.14 = (f32[192,256]{1,0:T(8,128)S(1)}, f32[192,256]{1,0:T(8,128)S(1)}, u32[]{:S(2)}, u32[]{:S(2)}) collective-permute-start(f32[192,256]{1,0:T(8,128)S(1)} %pad_maximum_fusion.1), channel_id=1, source_target_pairs={{0,2},{1,3},{2,0},{3,1},{4,6},{5,7},{6,4},{7,5},{8,10},{9,11},{10,... | collective-permute-start | bytes 589832 | tf_op jit(solution)/shard_map/ppermute | solution.py:237
  155.2 5.6 %collective-permute-start.22 = (f32[192,256]{1,0:T(8,128)S(1)}, f32[192,256]{1,0:T(8,128)S(1)}, u32[]{:S(2)}, u32[]{:S(2)}) collective-permute-start(f32[192,256]{1,0:T(8,128)S(1)} %pad_maximum_fusion.2), channel_id=1, source_target_pairs={{0,4},{4,0},{8,12},{12,8},{16,20},{20,16},{24,28},{28,24},{1,5},{5... | collective-permute-start | bytes 589832 | tf_op jit(solution)/shard_map/ppermute | solution.py:237
  161.0 18.0 %collective-permute-start.31 = (f32[1024,256]{1,0:T(8,128)S(1)}, f32[1024,256]{1,0:T(8,128)S(1)}, u32[]{:S(2)}, u32[]{:S(2)}) collective-permute-start(f32[1024,256]{1,0:T(8,128)S(1)} %select_dynamic-update-slice_fusion.4), channel_id=1, source_target_pairs={{0,1},{1,0},{2,3},{3,2},{4,5},{5,4},{6,7},{7,6},{8,9},{9,8},{10,11... | collective-permute-start | bytes 3145736 | tf_op jit(solution)/shard_map/ppermute | solution.py:237
  168.9 8.8 %collective-permute-start.3 = (f32[2,256,256]{2,1,0:T(8,128)S(1)}, f32[2,256,256]{2,1,0:T(8,128)S(1)}, u32[]{:S(2)}, u32[]{:S(2)}) collective-permute-start(f32[2,256,256]{2,1,0:T(8,128)S(1)} %copy-done.7), channel_id=1, source_target_pairs={{0,1},{1,2},{2,3},{4,5},{5,6},{6,7},{8,9},{9,10},{10,11},{12,13},{... | collective-permute-start | bytes 1572872 | tf_op jit(solution)/shard_map/ppermute | solution.py:232
  (11 other events, 111.1 us)

commit v2 on v1

v2 whole, which is shorter than its diff:
```python
import functools
import math

import jax
import jax.numpy as jnp
import ml_dtypes
import numpy as np
from jax import lax
from jax.experimental import pallas as pl
from jax.experimental.pallas import tpu as pltpu
from jax.sharding import PartitionSpec as P

F32 = jnp.float32
BF16 = jnp.bfloat16
LANES = 128


def half_dft(extent):
    half = extent // 2
    blocks = []
    for parity in range(2):
        freq = 2 * np.arange(half)[:, None] + parity
        angles = (freq * np.arange(half)[None, :] % extent) * (2.0 * math.pi / extent)
        cosine = np.cos(angles) / math.sqrt(extent)
        sine = np.sin(angles) / math.sqrt(extent)
        blocks.append(np.block([[cosine, sine], [-sine, cosine]]))
    both = np.stack(blocks)
    return np.stack([both, np.swapaxes(both, 1, 2)]).astype(ml_dtypes.bfloat16)


def parity_order(extent):
    order = np.concatenate([np.arange(0, extent, 2), np.arange(1, extent, 2)])
    matrix = np.zeros((extent, extent), np.float32)
    matrix[order, np.arange(extent)] = 1.0
    return matrix


def dot(a, b):
    return jnp.dot(a, b, preferred_element_type=F32)


def slots_kernel(
    late, tile_rows, tile_cols, offsets, live, *refs,
):
    pieces = refs[: 8 if late else 5]
    refs = refs[len(pieces) :]
    if late:
        grad_so_far, probe_so_far, probe, amps, mats, order = refs[:6]
        grad_own, grad_below, grad_right, grad_right_low, grad_corner, probe_keep, probe_send = refs[6:13]
        refs = refs[13:]
    else:
        probe, amps, mats, order, grad_out, probe_out = refs[:6]
        refs = refs[6:]
    ext, grad, probe_sum, window, part, amp, sorted_amp, waves, inner, far, power, across, in_sems, amp_sem, out_sems = refs
    modes = probe.shape[0]
    extent = probe.shape[2]
    half = extent // 2
    rows_step = 32
    groups = rows_step // 8
    count = live[0]

    low_rows = slice(tile_rows, tile_rows + extent)
    first = slice(tile_cols, tile_cols + LANES)
    second = slice(tile_cols + LANES, tile_cols + extent)
    places = [(slice(0, tile_rows), slice(0, tile_cols)), (low_rows, slice(0, tile_cols))]
    for cols in (first, second):
        places += [(slice(0, extent), cols), (slice(extent, tile_rows), cols), (low_rows, cols)]
    loads = [
        pltpu.make_async_copy(src, ext.at[:, rows, cols], in_sems.at[n])
        for n, (src, (rows, cols)) in enumerate(zip(pieces, places))
    ]
    if late:
        loads.append(pltpu.make_async_copy(grad_so_far, grad, in_sems.at[len(pieces)]))
        loads.append(pltpu.make_async_copy(probe_so_far, probe_sum, in_sems.at[len(pieces) + 1]))
    for load in loads:
        load.start()
    if not late:
        grad[...] = jnp.zeros_like(grad)
        probe_sum[...] = jnp.zeros_like(probe_sum)
    for load in loads:
        load.wait()
    lane = lax.broadcasted_iota(jnp.int32, (rows_step, LANES), 1)
    lane3 = lax.broadcasted_iota(jnp.int32, (groups + 1, 8, LANES), 2)
    sublane = lax.broadcasted_iota(jnp.int32, (groups, 8, LANES), 1)
    sublane_tall = lax.broadcasted_iota(jnp.int32, (groups + 1, 8, LANES), 1)

    def rows_of(k, c, rows):
        start = (k * 2 + c) * extent
        return slice(start + rows.start, start + rows.stop)

    def visit(number, row_at, col_at):
        amp_load = pltpu.make_async_copy(amps.at[number], amp, amp_sem)
        amp_load.start()
        shift = lax.rem(col_at, LANES)
        col_base = pl.multiple_of(col_at - shift, LANES)
        back = lax.rem(LANES - shift, LANES)
        wide_cols = extent // LANES + 1
        row_shift = lax.rem(row_at, 8)
        row_base = pl.multiple_of(row_at - row_shift, 8)
        row_back = lax.rem(8 - row_shift, 8)

        for plane in range(2):
            for row in range(0, extent, rows_step):
                turned = []
                for c in range(wide_cols):
                    tall = ext[plane, pl.ds(row_base + row, rows_step + 8), pl.ds(col_base + LANES * c, LANES)]
                    tall = pltpu.roll(tall.reshape(groups + 1, 8, LANES), row_back, 1)
                    flat = jnp.where(sublane < 8 - row_shift, tall[:-1], tall[1:]).reshape(rows_step, LANES)
                    turned.append(pltpu.roll(flat, back, 1))
                for c in range(wide_cols - 1):
                    window[plane, row : row + rows_step, c * LANES : (c + 1) * LANES] = jnp.where(
                        lane < LANES - shift, turned[c], turned[c + 1]
                    )


        def psi(k, step=rows_step):
            for row in range(0, half, step):
                waves_at = []
                for base in (row, half + row):
                    rows = slice(base, base + step)
                    pr, pi = probe[k, 0, rows, :], probe[k, 1, rows, :]
                    o_re, o_im = window[0, rows, :], window[1, rows, :]
                    waves_at.append((pr * o_re - pi * o_im, pr * o_im + pi * o_re))
                for c in range(2):
                    rows = slice(c * half + row, c * half + row + step)
                    waves[k, 0, rows, :] = (waves_at[0][c] + waves_at[1][c]).astype(BF16)
                    waves[k, 1, rows, :] = (waves_at[0][c] - waves_at[1][c]).astype(BF16)

        def left(k):
            for a in range(2):
                z = dot(mats[0, a], waves[k, a])
                left, right_half = z[:, :half], z[:, half:]
                for b, value in enumerate((left + right_half, left - right_half)):
                    value = value.astype(BF16)
                    inner[k, b, a * half : (a + 1) * half, :half] = value[:half]
                    inner[k, b, a * half : (a + 1) * half, half:] = value[half:]

        def right(k):
            for b in range(2):
                f = dot(inner[k, b], mats[1, b])
                far[k, b] = f
                own_power = f[:, :half] * f[:, :half] + f[:, half:] * f[:, half:]
                power[b] = own_power if k == 0 else power[b] + own_power

        def factors():
            amp_load.wait()
            high = amp[...].astype(BF16)
            low = (amp[...] - high.astype(F32)).astype(BF16)
            turned = dot(high, order[...]) + dot(low, order[...])
            for b in range(2):
                sorted_amp[b] = turned[:, b * half : (b + 1) * half]
            for b in range(2):
                for a in range(2):
                    rows = slice(a * half, (a + 1) * half)
                    for_rows = sorted_amp[b, pl.ds(a, half, 2), :]
                    power[b, rows] = 2.0 - 2.0 * for_rows * lax.rsqrt(power[b, rows] + 0.5)

        def back_right(k):
            ys = []
            for b in range(2):
                factor = power[b]
                g = jnp.concatenate([far[k, b, :, :half] * factor, far[k, b, :, half:] * factor], 1)
                ys.append(dot(g.astype(BF16), mats[0, b]))
            for side, y in enumerate((ys[0] + ys[1], ys[0] - ys[1])):
                y = y.astype(BF16)
                cols = slice(side * half, (side + 1) * half)
                for a in range(2):
                    rows = slice(a * half, (a + 1) * half)
                    across[k, a, :half, cols] = y[rows, :half]
                    across[k, a, half:, cols] = y[rows, half:]

        def back_left(k):
            v0 = dot(mats[1, 0], across[k, 0])
            v1 = dot(mats[1, 1], across[k, 1])
            for side, v in enumerate((v0 + v1, v0 - v1)):
                rows = slice(side * half, (side + 1) * half)
                g_re, g_im = v[:half], v[half:]
                pr, pi = probe[k, 0, rows, :], probe[k, 1, rows, :]
                o_re, o_im = window[0, rows, :], window[1, rows, :]
                add_re = pr * g_re + pi * g_im
                add_im = pr * g_im - pi * g_re
                part[0, rows, :] = add_re if k == 0 else part[0, rows, :] + add_re
                part[1, rows, :] = add_im if k == 0 else part[1, rows, :] + add_im
                probe_sum[rows_of(k, 0, rows), :] += o_re * g_re + o_im * g_im
                probe_sum[rows_of(k, 1, rows), :] += o_re * g_im - o_im * g_re

        for stage in (psi, left, right):
            for k in range(modes):
                stage(k)
        factors()
        for stage in (back_right, back_left):
            for k in range(modes):
                stage(k)

        zero = jnp.zeros((groups + 1, 8, LANES), F32)
        edge = jnp.zeros((1, 8, LANES), F32)
        for plane in range(2):
            for row in range(0, extent, rows_step):
                turned = []
                for c in range(wide_cols - 1):
                    flat = part[plane, row : row + rows_step, c * LANES : (c + 1) * LANES]
                    flat = pltpu.roll(flat, shift, 1).reshape(groups, 8, LANES)
                    flat = pltpu.roll(flat, row_shift, 1)
                    low = jnp.concatenate([flat, edge], 0)
                    high = jnp.concatenate([edge, flat], 0)
                    turned.append(jnp.where(sublane_tall >= row_shift, low, high))
                turned = [zero] + turned + [zero]
                for c in range(wide_cols):
                    at = (plane, pl.ds(row_base + row, rows_step + 8), pl.ds(col_base + LANES * c, LANES))
                    value = jnp.where(lane3 >= shift, turned[c + 1], turned[c])
                    grad[at] += value.reshape(rows_step + 8, LANES)

    @pl.loop(0, count)
    def _(number):
        row_at = lax.rem(offsets[number, 0], tile_rows)
        col_at = lax.rem(offsets[number, 1], tile_cols)

        @pl.when((col_at > LANES) == late)
        def _():
            visit(number, row_at, col_at)

    if late:
        own_half = (lax.axis_index("narrow") & 1) * (probe_sum.shape[0] // 2)
        other_half = probe_sum.shape[0] // 2 - own_half
        whole = slice(0, tile_cols)
        rim = slice(tile_cols, tile_cols + extent)
        pairs = [
            (probe_sum.at[pl.ds(pl.multiple_of(start, 8), probe_sum.shape[0] // 2), :], dst)
            for start, dst in ((other_half, probe_send), (own_half, probe_keep))
        ] + [
            (grad.at[:, low_rows, rim], grad_corner),
            (grad.at[:, low_rows, whole], grad_below),
            (grad.at[:, 0:extent, rim], grad_right),
            (grad.at[:, extent:tile_rows, rim], grad_right_low),
            (grad.at[:, 0:tile_rows, whole], grad_own),
        ]
    else:
        pairs = [(grad, grad_out), (probe_sum, probe_out)]
    stores = [pltpu.make_async_copy(src, dst, out_sems.at[n]) for n, (src, dst) in enumerate(pairs)]
    for store in stores:
        store.start()
    for store in stores:
        store.wait()


def run_slots(late, offsets, live, pieces, sums, probe, amps):
    extent = probe.shape[2]
    modes = probe.shape[0]
    tile_rows, tile_cols = pieces[0].shape[1:]
    mats = jnp.asarray(half_dft(extent))
    order = jnp.asarray(parity_order(extent)).astype(BF16)
    smem = pl.BlockSpec(memory_space=pltpu.SMEM)
    vmem = pl.BlockSpec(memory_space=pltpu.VMEM)
    hbm = pl.BlockSpec(memory_space=pl.ANY)
    grad_shape = (2, tile_rows + extent, tile_cols + extent)
    sum_shape = (modes * 2 * extent, extent)
    half_sum = (sum_shape[0] // 2, extent)
    if late:
        outs = [(2, tile_rows, tile_cols), (2, extent, tile_cols), (2, extent, extent), (2, tile_rows - extent, extent)]
        outs += [(2, extent, extent), half_sum, half_sum]
    else:
        outs = [grad_shape, sum_shape]
    return pl.pallas_call(
        functools.partial(slots_kernel, late, tile_rows, tile_cols),
        out_shape=[jax.ShapeDtypeStruct(shape, F32) for shape in outs],
        in_specs=[smem, smem] + [hbm] * (len(pieces) + len(sums)) + [vmem, hbm, vmem, vmem],
        out_specs=[hbm] * len(outs),
        scratch_shapes=[
            pltpu.VMEM(grad_shape, F32),
            pltpu.VMEM(grad_shape, F32),
            pltpu.VMEM(sum_shape, F32),
            pltpu.VMEM((2, extent, extent), F32),
            pltpu.VMEM((2, extent, extent), F32),
            pltpu.VMEM((extent, extent), F32),
            pltpu.VMEM((2, extent, extent // 2), F32),
            pltpu.VMEM((modes, 2, extent, extent), BF16),
            pltpu.VMEM((modes, 2, extent, extent), BF16),
            pltpu.VMEM((modes, 2, extent, extent), F32),
            pltpu.VMEM((2, extent, extent // 2), F32),
            pltpu.VMEM((modes, 2, extent, extent), BF16),
            pltpu.SemaphoreType.DMA((10,)),
            pltpu.SemaphoreType.DMA(()),
            pltpu.SemaphoreType.DMA((7,)),
        ],
        compiler_params=pltpu.CompilerParams(vmem_limit_bytes=40 * 1024 * 1024),
        name="late_slots" if late else "early_slots",
    )(offsets, live, *pieces, *sums, probe, amps, mats, order)


def split_kernel(extent, tile_rows, tile, *refs):
    outs, sems = refs[:-1], refs[-1]
    spans = []
    for cols in (slice(0, LANES), slice(LANES, extent)):
        spans += [(slice(0, extent), cols), (slice(extent, tile_rows), cols)]
    spans.append((slice(0, extent), slice(0, tile.shape[2])))
    copies = [
        pltpu.make_async_copy(tile.at[:, rows, cols], out, sems.at[n]) for n, ((rows, cols), out) in enumerate(zip(spans, outs))
    ]
    for copy in copies:
        copy.start()
    for copy in copies:
        copy.wait()


def split_tile(tile, extent):
    rows, cols = tile.shape[1:]
    shapes = [(2, extent, LANES), (2, rows - extent, LANES), (2, extent, extent - LANES), (2, rows - extent, extent - LANES)]
    shapes.append((2, extent, cols))
    hbm = pl.BlockSpec(memory_space=pl.ANY)
    return pl.pallas_call(
        functools.partial(split_kernel, extent, rows),
        out_shape=[jax.ShapeDtypeStruct(shape, F32) for shape in shapes],
        in_specs=[hbm],
        out_specs=[hbm] * len(shapes),
        scratch_shapes=[pltpu.SemaphoreType.DMA((len(shapes),))],
        name="split_tile",
    )(tile)


def shifted(value, axis, steps):
    count = lax.axis_size(axis)
    first, last = (max(0, -steps), min(count, count - steps))
    return lax.ppermute(value, axis, [(source, source + steps) for source in range(first, last)])


def place_in(bits):
    linear = lax.axis_index("wide") * lax.axis_size("narrow") + lax.axis_index("narrow")
    place = 0
    for n, bit in enumerate(bits):
        place = place + ((linear // bit) % 2) * (1 << n)
    return place


def partners(bits):
    return [sum(bit for n, bit in enumerate(bits) if step >> n & 1) for step in range(1 << len(bits))]


def swapped(value, mask):
    count = lax.axis_size("wide") * lax.axis_size("narrow")
    return lax.ppermute(value, ("wide", "narrow"), [(source, source ^ mask) for source in range(count)])


def add_kernel(bits, count, *refs):
    ins, outs = refs[:count], refs[count:]
    rows = outs[0].shape[0]
    place = place_in(bits)
    for step, out in enumerate(outs):
        at = pl.ds(pl.multiple_of((place ^ step) * rows, 8), rows)
        out[...] = sum(ref[at, :] for ref in ins)


def add_parts(parts, bits):
    count = 1 << len(bits)
    rows, cols = parts[0].shape
    vmem = pl.BlockSpec(memory_space=pltpu.VMEM)
    return pl.pallas_call(
        functools.partial(add_kernel, bits, len(parts)),
        out_shape=[jax.ShapeDtypeStruct((rows // count, cols), F32)] * count,
        in_specs=[vmem] * len(parts),
        out_specs=[vmem] * count,
        compiler_params=pltpu.CompilerParams(vmem_limit_bytes=8 * 1024 * 1024),
        name="add_parts",
    )(*parts)


def join_kernel(bits, scale, *refs):
    ins, out = refs[:-1], refs[-1]
    rows = ins[0].shape[0]
    place = place_in(bits)
    for step, ref in enumerate(ins):
        at = pl.ds(pl.multiple_of((place ^ step) * rows, 8), rows)
        out[at, :] = ref[...] if scale is None else ref[...] * scale


def join_parts(parts, bits, scale=None):
    rows, cols = parts[0].shape
    vmem = pl.BlockSpec(memory_space=pltpu.VMEM)
    return pl.pallas_call(
        functools.partial(join_kernel, bits, scale),
        out_shape=jax.ShapeDtypeStruct((rows * len(parts), cols), F32),
        in_specs=[vmem] * len(parts),
        out_specs=vmem,
        compiler_params=pltpu.CompilerParams(vmem_limit_bytes=8 * 1024 * 1024),
        name="join_parts",
    )(*parts)


def sum_everywhere(keep, send, scale):
    narrow, wide = lax.axis_size("narrow"), lax.axis_size("wide")
    bits = [1 << n for n in range((narrow * wide).bit_length() - 1)]
    groups = [tuple(bits[n : n + 2]) for n in range(1, len(bits), 2)]
    parts = [keep, swapped(send, bits[0])]
    for group in groups:
        pieces = add_parts(parts, group)
        parts = [pieces[0]] + [swapped(piece, mask) for piece, mask in zip(pieces[1:], partners(group)[1:])]
    value = add_parts(parts, ())[0]
    for group in reversed(groups):
        parts = [value] + [swapped(value, mask) for mask in partners(group)[1:]]
        if group != groups[0]:
            value = join_parts(parts, group)
    parts = parts + [swapped(part, bits[0]) for part in parts]
    return join_parts(parts, groups[0] + (bits[0],), scale)


def on_device(object_field, probe, amplitudes, offsets, live):
    extent = probe.shape[2]
    first_top, first_low, second_top, second_low, top = split_tile(object_field, extent)
    strips = [shifted(part, "wide", -1) for part in (first_top, first_low, second_top, second_low)]
    below = shifted(top, "narrow", -1)
    corner = shifted(strips[0], "narrow", -1)
    early = [object_field, below, strips[0], strips[1], corner]
    grad_so_far, probe_so_far = run_slots(False, offsets, live, early, [], probe, amplitudes)
    second, probe_so_far = lax.optimization_barrier((strips[2], probe_so_far))
    late = early + [second, strips[3], shifted(second, "narrow", -1)]
    grad_own, grad_below, grad_right, grad_right_low, grad_corner, keep, send = run_slots(
        True, offsets, live, late, [grad_so_far, probe_so_far], probe, amplitudes
    )
    came_corner = shifted(grad_corner, "narrow", 1)
    came_below = shifted(grad_below, "narrow", 1)
    came_right = shifted(grad_right + came_corner, "wide", 1)
    came_right_low = shifted(grad_right_low, "wide", 1)
    total_slots = lax.axis_size("wide") * lax.axis_size("narrow") * offsets.shape[0]
    probe_grad = sum_everywhere(keep, send, 1.0 / math.sqrt(total_slots)).reshape(probe.shape)
    rims = jnp.concatenate([came_right, came_right_low], 1)
    object_grad = grad_own.at[:, :extent, :].add(came_below).at[:, :, :extent].add(rims)
    return (object_grad, probe_grad)


def solution(mesh):
    return jax.shard_map(
        on_device,
        mesh=mesh,
        in_specs=(
            P(None, "narrow", "wide"),
            P(),
            P(("wide", "narrow"), None, None),
            P(("wide", "narrow"), None),
            P(("wide", "narrow")),
        ),
        out_specs=(P(None, "narrow", "wide"), P()),
        check_vma=False,
    )
```

time: 182 us -> 196 us (1.077)
  the two profiles are of different devices: /device:TPU:1 before, /device:TPU:0 now
where the time goes in v2:
time: 196 us; the launch traced here: 194 us
  starting transfers between devices  79 us (40%)
  Pallas kernels  59.5 us (30%)
  waiting for transfers between devices  44.3 us (23%)
  local copies, waits for them, and re-layouts  8.73 us (4%)
    ppermute x17, starting transfers between devices, swapped(): lax.ppermute(value, ('wide', 'narrow'), [(source, source ^ mask) for sour...  60.8 us
    pallas_call x1, Pallas kernels, split_tile(): pl.pallas_call(functools.partial(split_kernel, extent, rows), out_shape=[...  48.8 us
    ppermute x17, waiting for transfers between devices, swapped(): lax.ppermute(value, ('wide', 'narrow'), [(source, source ^ mask) for sour...  31.7 us
    ppermute x11, starting transfers between devices, shifted(): lax.ppermute(value, axis, [(source, source + steps) for source in range(f...  18.1 us
    ppermute x11, waiting for transfers between devices, shifted(): lax.ppermute(value, axis, [(source, source + steps) for source in range(f...  12.6 us
    pallas_call x2, Pallas kernels, run_slots(): pl.pallas_call(functools.partial(slots_kernel, late, tile_rows, tile_cols...  9.01 us
    unnamed x13, local copies, waits for them, and re-layouts  8.73 us
  transfers between devices with their start and end apart: 28, of which 16 were waited for; matrix products, arithmetic and copies ran while one was open for 1% of the time, Pallas kernels for 1%

profile of v2, /device:TPU:0, one launch (start us, length us, event | category | flops | bytes accessed | tf_op | source)
XLA Modules:
  0.0 194.4 jit_solution(10115895281567551799)
XLA Ops:
  0.6 48.8 %split_tile.1 = (f32[2,256,128]{2,1,0:T(8,128)}, f32[2,256,128]{2,1,0:T(8,128)}, f32[2,256,128]{2,1,0:T(8,128)}, f32[2,256,128]{2,1,0:T(8,128)}, f32[2,256,256]{2,1,0:T(8,128)}) custom-call(f32[2,512,256]{2,1,0:T(8,128)} %refs_0_.3), custom_call_target="tpu_custom_call" | custom-call | tf_op jit(solution)/shard_map/split_tile/pallas_call | solution.py:310
  49.4 1.3 collective-permute-start.1
  50.7 1.3 collective-permute-start
  53.3 8.3 %collective-permute-done.1.refs_2_ = f32[2,256,128]{2,1,0:T(8,128)S(1)} collective-permute-done((f32[2,256,128]{2,1,0:T(8,128)}, f32[2,256,128]{2,1,0:T(8,128)S(1)}, u32[]{:S(2)}, u32[]{:S(2)}) %collective-permute-start.1) | collective-permute-done | bytes 262176 | tf_op jit(solution)/shard_map/ppermute | solution.py:323
  68.1 1.6 copy-done.1
  69.7 1.6 copy-done.2
  73.3 1.8 early_slots.1
  75.1 1.6 copy-done.3
  78.0 2.0 %collective-permute-done.5.refs_6_ = f32[2,256,128]{2,1,0:T(8,128)S(1)} collective-permute-done((f32[2,256,128]{2,1,0:T(8,128)}, f32[2,256,128]{2,1,0:T(8,128)S(1)}, u32[]{:S(2)}, u32[]{:S(2)}) %collective-permute-start.5) | collective-permute-done | bytes 262176 | tf_op jit(solution)/shard_map/ppermute | solution.py:323
  80.0 2.4 %collective-permute-done.6.refs_7_ = f32[2,256,128]{2,1,0:T(8,128)S(1)} collective-permute-done((f32[2,256,128]{2,1,0:T(8,128)S(1)}, f32[2,256,128]{2,1,0:T(8,128)S(1)}, u32[]{:S(2)}, u32[]{:S(2)}) %collective-permute-start.6) | collective-permute-done | bytes 262176 | tf_op jit(solution)/shard_map/ppermute | solution.py:323
  82.4 7.2 %late_slots.1 = (f32[2,512,256]{2,1,0:T(8,128)S(1)}, f32[2,256,256]{2,1,0:T(8,128)S(1)}, f32[2,256,256]{2,1,0:T(8,128)S(1)}, f32[2,256,256]{2,1,0:T(8,128)S(1)},...) custom-call(s32[8,2]{1,0:T(8,128)S(1)} %copy.12.offsets, s32[1]{0:T(128)S(6)} %copy.14.live, ...), custom_call_target="tpu_custom_call" | custom-call | tf_op jit(solution)/shard_map/late_slots/pallas_call | solution.py:263
  89.6 9.8 %collective-permute-start.11 = (f32[1024,256]{1,0:T(8,128)S(1)}, f32[1024,256]{1,0:T(8,128)S(1)}, u32[]{:S(2)}, u32[]{:S(2)}) collective-permute-start(f32[1024,256]{1,0:T(8,128)S(1)} %get-tuple-element.73), channel_id=1, source_target_pairs={{0,1},{1,0},{2,3},{3,2},{4,5},{5,4},{6,7},{7,6},{8,9},{9,8},{10,11... | collective-permute-start | bytes 3145736 | tf_op jit(solution)/shard_map/ppermute | solution.py:340
  99.4 1.9 %collective-permute-start.8 = (f32[2,256,256]{2,1,0:T(8,128)S(1)}, f32[2,256,256]{2,1,0:T(8,128)S(1)}, u32[]{:S(2)}, u32[]{:S(2)}) collective-permute-start(f32[2,256,256]{2,1,0:T(8,128)S(1)} %get-tuple-element.70), channel_id=1, source_target_pairs={{0,1},{1,2},{2,3},{4,5},{5,6},{6,7},{8,9},{9,10},{10,11},{12,13},{... | collective-permute-start | bytes 1572872 | tf_op jit(solution)/shard_map/ppermute | solution.py:323
  101.8 3.7 %collective-permute-start.12 = (f32[256,256]{1,0:T(8,128)S(1)}, f32[256,256]{1,0:T(8,128)S(1)}, u32[]{:S(2)}, u32[]{:S(2)}) collective-permute-start(f32[256,256]{1,0:T(8,128)S(1)} %get-tuple-element.75), channel_id=1, source_target_pairs={{0,2},{1,3},{2,0},{3,1},{4,6},{5,7},{6,4},{7,5},{8,10},{9,11},{10,... | collective-permute-start | bytes 786440 | tf_op jit(solution)/shard_map/ppermute | solution.py:340
  106.2 1.4 collective-permute-start.14
  107.6 1.8 collective-permute-start.7
  109.5 3.1 %collective-permute-done.12.refs_1_ = f32[256,256]{1,0:T(8,128)S(1)} collective-permute-done((f32[256,256]{1,0:T(8,128)S(1)}, f32[256,256]{1,0:T(8,128)S(1)}, u32[]{:S(2)}, u32[]{:S(2)}) %collective-permute-start.12) | collective-permute-done | bytes 262176 | tf_op jit(solution)/shard_map/ppermute | solution.py:340
  112.6 2.1 %collective-permute-done.13.refs_2_ = f32[256,256]{1,0:T(8,128)S(1)} collective-permute-done((f32[256,256]{1,0:T(8,128)S(1)}, f32[256,256]{1,0:T(8,128)S(1)}, u32[]{:S(2)}, u32[]{:S(2)}) %collective-permute-start.13) | collective-permute-done | bytes 262176 | tf_op jit(solution)/shard_map/ppermute | solution.py:340
  114.7 5.2 %collective-permute-done.14.refs_3_ = f32[256,256]{1,0:T(8,128)S(1)} collective-permute-done((f32[256,256]{1,0:T(8,128)S(1)}, f32[256,256]{1,0:T(8,128)S(1)}, u32[]{:S(2)}, u32[]{:S(2)}) %collective-permute-start.14) | collective-permute-done | bytes 262176 | tf_op jit(solution)/shard_map/ppermute | solution.py:340
  120.0 18.8 %collective-permute-start.15 = (f32[64,256]{1,0:T(8,128)S(1)}, f32[64,256]{1,0:T(8,128)S(1)}, u32[]{:S(2)}, u32[]{:S(2)}) collective-permute-start(f32[64,256]{1,0:T(8,128)S(1)} %get-tuple-element.79), channel_id=1, source_target_pairs={{0,8},{1,9},{2,10},{3,11},{4,12},{5,13},{6,14},{7,15},{8,0},{9,1},... | collective-permute-start | bytes 196616 | tf_op jit(solution)/shard_map/ppermute | solution.py:340
  138.8 1.7 collective-permute-start.10
  140.6 3.6 %collective-permute-start.9 = (f32[2,256,256]{2,1,0:T(8,128)S(1)}, f32[2,256,256]{2,1,0:T(8,128)S(1)}, u32[]{:S(2)}, u32[]{:S(2)}) collective-permute-start(f32[2,256,256]{2,1,0:T(8,128)S(1)} %add.20), channel_id=1, source_target_pairs={{0,4},{4,8},{8,12},{12,16},{16,20},{20,24},{24,28},{1,5},{5,9},{9,... | collective-permute-start | bytes 1572872 | tf_op jit(solution)/shard_map/ppermute | solution.py:323
  145.2 4.3 %collective-permute-done.16.refs_2_ = f32[64,256]{1,0:T(8,128)S(1)} collective-permute-done((f32[64,256]{1,0:T(8,128)S(1)}, f32[64,256]{1,0:T(8,128)S(1)}, u32[]{:S(2)}, u32[]{:S(2)}) %collective-permute-start.16) | collective-permute-done | bytes 65568 | tf_op jit(solution)/shard_map/ppermute | solution.py:340
  151.8 2.6 %collective-permute-start.19 = (f32[64,256]{1,0:T(8,128)S(1)}, f32[64,256]{1,0:T(8,128)S(1)}, u32[]{:S(2)}, u32[]{:S(2)}) collective-permute-start(f32[64,256]{1,0:T(8,128)S(1)} %add_parts.5.refs_0_), channel_id=1, source_target_pairs={{0,16},{1,17},{2,18},{3,19},{4,20},{5,21},{6,22},{7,23},{8,24},{9,... | collective-permute-start | bytes 196616 | tf_op jit(solution)/shard_map/ppermute | solution.py:340
  154.4 2.5 %collective-permute-done.20.refs_3_ = f32[64,256]{1,0:T(8,128)S(1)} collective-permute-done((f32[64,256]{1,0:T(8,128)S(1)}, f32[64,256]{1,0:T(8,128)S(1)}, u32[]{:S(2)}, u32[]{:S(2)}) %collective-permute-start.20) | collective-permute-done | bytes 65568 | tf_op jit(solution)/shard_map/ppermute | solution.py:340
  156.9 3.8 %collective-permute-start.18 = (f32[64,256]{1,0:T(8,128)S(1)}, f32[64,256]{1,0:T(8,128)S(1)}, u32[]{:S(2)}, u32[]{:S(2)}) collective-permute-start(f32[64,256]{1,0:T(8,128)S(1)} %add_parts.5.refs_0_), channel_id=1, source_target_pairs={{0,8},{1,9},{2,10},{3,11},{4,12},{5,13},{6,14},{7,15},{8,0},{9,1},... | collective-permute-start | bytes 196616 | tf_op jit(solution)/shard_map/ppermute | solution.py:340
  161.4 1.5 collective-permute-done.18.refs_1_
  163.0 15.9 %collective-permute-start.23 = (f32[256,256]{1,0:T(8,128)S(1)}, f32[256,256]{1,0:T(8,128)S(1)}, u32[]{:S(2)}, u32[]{:S(2)}) collective-permute-start(f32[256,256]{1,0:T(8,128)S(1)} %join_parts.2.refs_0_), channel_id=1, source_target_pairs={{0,6},{1,7},{2,4},{3,5},{4,2},{5,3},{6,0},{7,1},{8,14},{9,15},{10,... | collective-permute-start | bytes 786440 | tf_op jit(solution)/shard_map/ppermute | solution.py:340
  178.9 1.4 collective-permute-start.21
  180.5 5.5 %collective-permute-done.23.refs_3_ = f32[256,256]{1,0:T(8,128)S(1)} collective-permute-done((f32[256,256]{1,0:T(8,128)S(1)}, f32[256,256]{1,0:T(8,128)S(1)}, u32[]{:S(2)}, u32[]{:S(2)}) %collective-permute-start.23) | collective-permute-done | bytes 262176 | tf_op jit(solution)/shard_map/ppermute | solution.py:340
  186.0 4.9 %collective-permute-done.22.refs_2_ = f32[256,256]{1,0:T(8,128)S(1)} collective-permute-done((f32[256,256]{1,0:T(8,128)S(1)}, f32[256,256]{1,0:T(8,128)S(1)}, u32[]{:S(2)}, u32[]{:S(2)}) %collective-permute-start.22) | collective-permute-done | bytes 262176 | tf_op jit(solution)/shard_map/ppermute | solution.py:340
  192.9 1.5 join_parts.3
  (48 shorter events, 17.8 us)
Async XLA Ops:
  49.4 12.2 %collective-permute-start.1 = (f32[2,256,128]{2,1,0:T(8,128)}, f32[2,256,128]{2,1,0:T(8,128)S(1)}, u32[]{:S(2)}, u32[]{:S(2)}) collective-permute-start(f32[2,256,128]{2,1,0:T(8,128)} %get-tuple-element.59), channel_id=1, source_target_pairs={{4,0},{8,4},{12,8},{16,12},{20,16},{24,20},{28,24},{5,1},{9,5},{13... | collective-permute-start | bytes 786440 | tf_op jit(solution)/shard_map/ppermute | solution.py:323
  50.7 16.2 %collective-permute-start = (f32[2,256,256]{2,1,0:T(8,128)}, f32[2,256,256]{2,1,0:T(8,128)S(1)}, u32[]{:S(2)}, u32[]{:S(2)}) collective-permute-start(f32[2,256,256]{2,1,0:T(8,128)} %get-tuple-element.58), channel_id=1, source_target_pairs={{1,0},{2,1},{3,2},{5,4},{6,5},{7,6},{9,8},{10,9},{11,10},{13,12},{... | collective-permute-start | bytes 1572872 | tf_op jit(solution)/shard_map/ppermute | solution.py:323
  52.0 14.9 %collective-permute-start.2 = (f32[2,256,128]{2,1,0:T(8,128)}, f32[2,256,128]{2,1,0:T(8,128)S(1)}, u32[]{:S(2)}, u32[]{:S(2)}) collective-permute-start(f32[2,256,128]{2,1,0:T(8,128)} %get-tuple-element.60), channel_id=1, source_target_pairs={{4,0},{8,4},{12,8},{16,12},{20,16},{24,20},{28,24},{5,1},{9,5},{13... | collective-permute-start | bytes 786440 | tf_op jit(solution)/shard_map/ppermute | solution.py:323
  61.6 5.3 %collective-permute-start.3 = (f32[2,256,128]{2,1,0:T(8,128)S(1)}, f32[2,256,128]{2,1,0:T(8,128)S(1)}, u32[]{:S(2)}, u32[]{:S(2)}) collective-permute-start(f32[2,256,128]{2,1,0:T(8,128)S(1)} %collective-permute-done.1.refs_2_), channel_id=1, source_target_pairs={{1,0},{2,1},{3,2},{5,4},{6,5},{7,6},{9,8},{10,9},{11,10},{13,12},{... | collective-permute-start | bytes 786440 | tf_op jit(solution)/shard_map/ppermute | solution.py:323
  62.9 13.8 %collective-permute-start.4 = (f32[2,256,128]{2,1,0:T(8,128)}, f32[2,256,128]{2,1,0:T(8,128)S(1)}, u32[]{:S(2)}, u32[]{:S(2)}) collective-permute-start(f32[2,256,128]{2,1,0:T(8,128)} %get-tuple-element.61), channel_id=1, source_target_pairs={{4,0},{8,4},{12,8},{16,12},{20,16},{24,20},{28,24},{5,1},{9,5},{13... | collective-permute-start | bytes 786440 | tf_op jit(solution)/shard_map/ppermute | solution.py:323
  64.2 15.8 %collective-permute-start.5 = (f32[2,256,128]{2,1,0:T(8,128)}, f32[2,256,128]{2,1,0:T(8,128)S(1)}, u32[]{:S(2)}, u32[]{:S(2)}) collective-permute-start(f32[2,256,128]{2,1,0:T(8,128)} %get-tuple-element.64), channel_id=1, source_target_pairs={{4,0},{8,4},{12,8},{16,12},{20,16},{24,20},{28,24},{5,1},{9,5},{13... | collective-permute-start | bytes 786440 | tf_op jit(solution)/shard_map/ppermute | solution.py:323
  66.9 1.2 copy-start
  68.1 1.6 copy-start.1
  69.7 1.6 copy-start.2
  75.1 1.6 copy-start.3
  76.7 5.6 %collective-permute-start.6 = (f32[2,256,128]{2,1,0:T(8,128)S(1)}, f32[2,256,128]{2,1,0:T(8,128)S(1)}, u32[]{:S(2)}, u32[]{:S(2)}) collective-permute-start(f32[2,256,128]{2,1,0:T(8,128)S(1)} %collective-permute-done.4.refs_5_), channel_id=1, source_target_pairs={{1,0},{2,1},{3,2},{5,4},{6,5},{7,6},{9,8},{10,9},{11,10},{13,12},{... | collective-permute-start | bytes 786440 | tf_op jit(solution)/shard_map/ppermute | solution.py:323
  89.6 12.1 %collective-permute-start.11 = (f32[1024,256]{1,0:T(8,128)S(1)}, f32[1024,256]{1,0:T(8,128)S(1)}, u32[]{:S(2)}, u32[]{:S(2)}) collective-permute-start(f32[1024,256]{1,0:T(8,128)S(1)} %get-tuple-element.73), channel_id=1, source_target_pairs={{0,1},{1,0},{2,3},{3,2},{4,5},{5,4},{6,7},{7,6},{8,9},{9,8},{10,11... | collective-permute-start | bytes 3145736 | tf_op jit(solution)/shard_map/ppermute | solution.py:340
  99.4 41.1 %collective-permute-start.8 = (f32[2,256,256]{2,1,0:T(8,128)S(1)}, f32[2,256,256]{2,1,0:T(8,128)S(1)}, u32[]{:S(2)}, u32[]{:S(2)}) collective-permute-start(f32[2,256,256]{2,1,0:T(8,128)S(1)} %get-tuple-element.70), channel_id=1, source_target_pairs={{0,1},{1,2},{2,3},{4,5},{5,6},{6,7},{8,9},{9,10},{10,11},{12,13},{... | collective-permute-start | bytes 1572872 | tf_op jit(solution)/shard_map/ppermute | solution.py:323
  101.8 10.8 %collective-permute-start.12 = (f32[256,256]{1,0:T(8,128)S(1)}, f32[256,256]{1,0:T(8,128)S(1)}, u32[]{:S(2)}, u32[]{:S(2)}) collective-permute-start(f32[256,256]{1,0:T(8,128)S(1)} %get-tuple-element.75), channel_id=1, source_target_pairs={{0,2},{1,3},{2,0},{3,1},{4,6},{5,7},{6,4},{7,5},{8,10},{9,11},{10,... | collective-permute-start | bytes 786440 | tf_op jit(solution)/shard_map/ppermute | solution.py:340
  105.5 9.2 %collective-permute-start.13 = (f32[256,256]{1,0:T(8,128)S(1)}, f32[256,256]{1,0:T(8,128)S(1)}, u32[]{:S(2)}, u32[]{:S(2)}) collective-permute-start(f32[256,256]{1,0:T(8,128)S(1)} %get-tuple-element.76), channel_id=1, source_target_pairs={{0,4},{1,5},{2,6},{3,7},{4,0},{5,1},{6,2},{7,3},{8,12},{9,13},{10,... | collective-permute-start | bytes 786440 | tf_op jit(solution)/shard_map/ppermute | solution.py:340
  106.2 13.7 %collective-permute-start.14 = (f32[256,256]{1,0:T(8,128)S(1)}, f32[256,256]{1,0:T(8,128)S(1)}, u32[]{:S(2)}, u32[]{:S(2)}) collective-permute-start(f32[256,256]{1,0:T(8,128)S(1)} %get-tuple-element.77), channel_id=1, source_target_pairs={{0,6},{1,7},{2,4},{3,5},{4,2},{5,3},{6,0},{7,1},{8,14},{9,15},{10,... | collective-permute-start | bytes 786440 | tf_op jit(solution)/shard_map/ppermute | solution.py:340
  107.6 71.3 %collective-permute-start.7 = (f32[2,256,256]{2,1,0:T(8,128)S(1)}, f32[2,256,256]{2,1,0:T(8,128)S(1)}, u32[]{:S(2)}, u32[]{:S(2)}) collective-permute-start(f32[2,256,256]{2,1,0:T(8,128)S(1)} %get-tuple-element.68), channel_id=1, source_target_pairs={{0,1},{1,2},{2,3},{4,5},{5,6},{6,7},{8,9},{9,10},{10,11},{12,13},{... | collective-permute-start | bytes 1572872 | tf_op jit(solution)/shard_map/ppermute | solution.py:323
  120.0 24.3 %collective-permute-start.15 = (f32[64,256]{1,0:T(8,128)S(1)}, f32[64,256]{1,0:T(8,128)S(1)}, u32[]{:S(2)}, u32[]{:S(2)}) collective-permute-start(f32[64,256]{1,0:T(8,128)S(1)} %get-tuple-element.79), channel_id=1, source_target_pairs={{0,8},{1,9},{2,10},{3,11},{4,12},{5,13},{6,14},{7,15},{8,0},{9,1},... | collective-permute-start | bytes 196616 | tf_op jit(solution)/shard_map/ppermute | solution.py:340
  138.8 41.6 %collective-permute-start.10 = (f32[2,256,256]{2,1,0:T(8,128)S(1)}, f32[2,256,256]{2,1,0:T(8,128)S(1)}, u32[]{:S(2)}, u32[]{:S(2)}) collective-permute-start(f32[2,256,256]{2,1,0:T(8,128)S(1)} %get-tuple-element.71), channel_id=1, source_target_pairs={{0,4},{4,8},{8,12},{12,16},{16,20},{20,24},{24,28},{1,5},{5,9},{9,... | collective-permute-start | bytes 1572872 | tf_op jit(solution)/shard_map/ppermute | solution.py:323
  140.6 50.9 %collective-permute-start.9 = (f32[2,256,256]{2,1,0:T(8,128)S(1)}, f32[2,256,256]{2,1,0:T(8,128)S(1)}, u32[]{:S(2)}, u32[]{:S(2)}) collective-permute-start(f32[2,256,256]{2,1,0:T(8,128)S(1)} %add.20), channel_id=1, source_target_pairs={{0,4},{4,8},{8,12},{12,16},{16,20},{20,24},{24,28},{1,5},{5,9},{9,... | collective-permute-start | bytes 1572872 | tf_op jit(solution)/shard_map/ppermute | solution.py:323
  144.2 5.3 %collective-permute-start.16 = (f32[64,256]{1,0:T(8,128)S(1)}, f32[64,256]{1,0:T(8,128)S(1)}, u32[]{:S(2)}, u32[]{:S(2)}) collective-permute-start(f32[64,256]{1,0:T(8,128)S(1)} %get-tuple-element.80), channel_id=1, source_target_pairs={{0,16},{1,17},{2,18},{3,19},{4,20},{5,21},{6,22},{7,23},{8,24},{9,... | collective-permute-start | bytes 196616 | tf_op jit(solution)/shard_map/ppermute | solution.py:340
  144.3 6.2 %collective-permute-start.17 = (f32[64,256]{1,0:T(8,128)S(1)}, f32[64,256]{1,0:T(8,128)S(1)}, u32[]{:S(2)}, u32[]{:S(2)}) collective-permute-start(f32[64,256]{1,0:T(8,128)S(1)} %get-tuple-element.81), channel_id=1, source_target_pairs={{0,24},{1,25},{2,26},{3,27},{4,28},{5,29},{6,30},{7,31},{8,16},{9,... | collective-permute-start | bytes 196616 | tf_op jit(solution)/shard_map/ppermute | solution.py:340
  150.5 6.3 %collective-permute-start.20 = (f32[64,256]{1,0:T(8,128)S(1)}, f32[64,256]{1,0:T(8,128)S(1)}, u32[]{:S(2)}, u32[]{:S(2)}) collective-permute-start(f32[64,256]{1,0:T(8,128)S(1)} %add_parts.5.refs_0_), channel_id=1, source_target_pairs={{0,24},{1,25},{2,26},{3,27},{4,28},{5,29},{6,30},{7,31},{8,16},{9,... | collective-permute-start | bytes 196616 | tf_op jit(solution)/shard_map/ppermute | solution.py:340
  151.8 9.6 %collective-permute-start.19 = (f32[64,256]{1,0:T(8,128)S(1)}, f32[64,256]{1,0:T(8,128)S(1)}, u32[]{:S(2)}, u32[]{:S(2)}) collective-permute-start(f32[64,256]{1,0:T(8,128)S(1)} %add_parts.5.refs_0_), channel_id=1, source_target_pairs={{0,16},{1,17},{2,18},{3,19},{4,20},{5,21},{6,22},{7,23},{8,24},{9,... | collective-permute-start | bytes 196616 | tf_op jit(solution)/shard_map/ppermute | solution.py:340
  156.9 6.0 %collective-permute-start.18 = (f32[64,256]{1,0:T(8,128)S(1)}, f32[64,256]{1,0:T(8,128)S(1)}, u32[]{:S(2)}, u32[]{:S(2)}) collective-permute-start(f32[64,256]{1,0:T(8,128)S(1)} %add_parts.5.refs_0_), channel_id=1, source_target_pairs={{0,8},{1,9},{2,10},{3,11},{4,12},{5,13},{6,14},{7,15},{8,0},{9,1},... | collective-permute-start | bytes 196616 | tf_op jit(solution)/shard_map/ppermute | solution.py:340
  163.0 23.1 %collective-permute-start.23 = (f32[256,256]{1,0:T(8,128)S(1)}, f32[256,256]{1,0:T(8,128)S(1)}, u32[]{:S(2)}, u32[]{:S(2)}) collective-permute-start(f32[256,256]{1,0:T(8,128)S(1)} %join_parts.2.refs_0_), channel_id=1, source_target_pairs={{0,6},{1,7},{2,4},{3,5},{4,2},{5,3},{6,0},{7,1},{8,14},{9,15},{10,... | collective-permute-start | bytes 786440 | tf_op jit(solution)/shard_map/ppermute | solution.py:340
  178.9 12.1 %collective-permute-start.22 = (f32[256,256]{1,0:T(8,128)S(1)}, f32[256,256]{1,0:T(8,128)S(1)}, u32[]{:S(2)}, u32[]{:S(2)}) collective-permute-start(f32[256,256]{1,0:T(8,128)S(1)} %join_parts.2.refs_0_), channel_id=1, source_target_pairs={{0,4},{1,5},{2,6},{3,7},{4,0},{5,1},{6,2},{7,3},{8,12},{9,13},{10,... | collective-permute-start | bytes 786440 | tf_op jit(solution)/shard_map/ppermute | solution.py:340
  178.9 12.2 %collective-permute-start.21 = (f32[256,256]{1,0:T(8,128)S(1)}, f32[256,256]{1,0:T(8,128)S(1)}, u32[]{:S(2)}, u32[]{:S(2)}) collective-permute-start(f32[256,256]{1,0:T(8,128)S(1)} %join_parts.2.refs_0_), channel_id=1, source_target_pairs={{0,2},{1,3},{2,0},{3,1},{4,6},{5,7},{6,4},{7,5},{8,10},{9,11},{10,... | collective-permute-start | bytes 786440 | tf_op jit(solution)/shard_map/ppermute | solution.py:340
  180.4 12.2 %collective-permute-start.24 = (f32[256,256]{1,0:T(8,128)S(1)}, f32[256,256]{1,0:T(8,128)S(1)}, u32[]{:S(2)}, u32[]{:S(2)}) collective-permute-start(f32[256,256]{1,0:T(8,128)S(1)} %join_parts.2.refs_0_), channel_id=1, source_target_pairs={{0,1},{1,0},{2,3},{3,2},{4,5},{5,4},{6,7},{7,6},{8,9},{9,8},{10,11... | collective-permute-start | bytes 786440 | tf_op jit(solution)/shard_map/ppermute | solution.py:340
  186.0 6.6 %collective-permute-start.27 = (f32[256,256]{1,0:T(8,128)S(1)}, f32[256,256]{1,0:T(8,128)S(1)}, u32[]{:S(2)}, u32[]{:S(2)}) collective-permute-start(f32[256,256]{1,0:T(8,128)S(1)} %collective-permute-done.23.refs_3_), channel_id=1, source_target_pairs={{0,1},{1,0},{2,3},{3,2},{4,5},{5,4},{6,7},{7,6},{8,9},{9,8},{10,11... | collective-permute-start | bytes 786440 | tf_op jit(solution)/shard_map/ppermute | solution.py:340
  191.0 1.7 collective-permute-start.26
  191.1 1.8 collective-permute-start.25
  (2 other events, 1.9 us)
